TPU v7x, 256 devices: a whole 4x4x8 slice. The times are simulated.
256 devices in a mesh: seq: 2 (over core), dp: 128 (over z, y, x).
Axes of the slice: x: 4, y: 4, z: 8, core: 2. Of those that a mesh axis runs over, the one named last changes fastest.
Arguments:
- hidden: bfloat16 [128, 512, 2560], P('dp', 'seq'), may hold values from -6 to 6
- scan_input: bfloat16 [128, 512, 2560], P('dp', 'seq'), may hold values from -6 to 6
- grad_out: bfloat16 [128, 512, 2560], P('dp', 'seq'), may hold values from -6 to 6
- step_size: float32 [128, 40, 512], P('dp', None, 'seq'), may hold values from 0.5 to 400
- proj_weight: bfloat16 [2560, 256], replicated, may hold values from -0.0068359375 to 0.0068359375
- log_rate: float32 [40], replicated, may hold values from -7.825 to -3.506
- skip_gain: float32 [40], replicated, may hold values from 0.5 to 1.5
- tile_list: int32 [128, 2], P('dp', 'seq'), may hold values from 0 to 1, as said below
Outputs:
- grad_input: bfloat16 [128, 512, 2560], P('dp', 'seq')
- grad_step: float32 [128, 40, 512], P('dp', None, 'seq')
- grad_weight: float32 [2560, 256], P('seq')
- grad_rate: float32 [40], P('seq')
- grad_skip: float32 [40], P('seq')
Inputs may be any that keep to these rules, and one draw needn't show every extreme that they name: `tile_list`: for each device, its 1 entries list the local indices of its valid groups in increasing order, then 1 in every unused entry; in every draw some device has the one group valid.
All inputs are finite; a program needn't handle non-finite values.
Results may differ from a plain program's by a relative error of at most 0.003.
Values sent between devices are 32-bit elements; how exact they have to be, the bound alone decides.
No kernel may reach another device: no remote copies, remote signals or barrier semaphores. Data moves between devices by JAX's collectives and lax.ppermute only.
A program may use at most 192 MiB of HBM per device.

v0:
```python
import jax
import jax.numpy as jnp
from jax import lax
from jax.sharding import PartitionSpec as P

exact_mode = lax.Precision.HIGHEST


def from_behind(x, axis, by):
    peers = lax.axis_size(axis)
    pairs = [(i, i + by) for i in range(peers) if 0 <= i + by < peers]
    return lax.ppermute(x, axis, pairs)


def group_forward(
    carry_state, group_values, group_keys, group_query, group_step, decay_rate, gain_vector
):
    block_len = group_values.shape[0]
    log_steps = group_step * decay_rate[:, None]
    running = jnp.cumsum(log_steps, axis=1)
    row_index = lax.broadcasted_iota(jnp.int32, (block_len, block_len), 0)
    col_index = lax.broadcasted_iota(jnp.int32, (block_len, block_len), 1)
    causal = row_index >= col_index
    spread = running[:, :, None] - running[:, None, :]
    decays = jnp.exp(jnp.where(causal[None], spread, -jnp.inf))
    scores = jnp.einsum("in,jn->ij", group_query, group_keys, precision=exact_mode)
    mixing = decays * scores[None] * group_step[:, None, :]
    within = jnp.einsum("hij,jhp->ihp", mixing, group_values, precision=exact_mode)
    carried = (
        jnp.einsum("in,hpn->ihp", group_query, carry_state, precision=exact_mode)
        * jnp.exp(running).T[:, :, None]
    )
    output = within + carried + gain_vector[None, :, None] * group_values
    tail_weight = jnp.exp(running[:, -1:] - running) * group_step
    weighted = group_values * tail_weight.T[:, :, None]
    fresh_state = jnp.einsum("jhp,jn->hpn", weighted, group_keys, precision=exact_mode)
    new_state = jnp.exp(running[:, -1])[:, None, None] * carry_state + fresh_state
    return (new_state, output)


def pass_group(
    carry_state, group_values, group_keys, group_query, group_step, decay_rate, gain_vector
):
    return (carry_state, jnp.zeros_like(group_values))


def group_tail(carry_state, group_values, group_keys, group_step, decay_rate):
    running = jnp.cumsum(group_step * decay_rate[:, None], axis=1)
    tail_weight = jnp.exp(running[:, -1:] - running) * group_step
    weighted = group_values * tail_weight.T[:, :, None]
    fresh_state = jnp.einsum("jhp,jn->hpn", weighted, group_keys, precision=exact_mode)
    return jnp.exp(running[:, -1])[:, None, None] * carry_state + fresh_state


def keep_state(carry_state, group_values, group_keys, group_step, decay_rate):
    return carry_state


def pull_group(before, group_query, group_grad, group_logs):
    running = jnp.cumsum(group_logs, axis=1)
    scaled = group_grad * jnp.exp(running).T[:, :, None]
    return jnp.einsum("qhp,qn->hpn", scaled, group_query, precision=exact_mode)


def empty_pull(before, group_query, group_grad, group_logs):
    return jnp.zeros((group_grad.shape[1], group_grad.shape[2], group_query.shape[1]), jnp.float32)


def shards(hidden, scan_input, grad_out, step_size, proj_weight, log_rate, skip_gain, tile_list):
    token_count = hidden.shape[1]
    group_total = tile_list.shape[1]
    block_len = token_count // group_total
    head_count = log_rate.shape[0]
    head_width = scan_input.shape[2] // head_count
    state_width = proj_weight.shape[1] // 2
    slot_ids = jnp.arange(group_total, dtype=jnp.int32)
    present = jnp.any(tile_list[0][:, None] == slot_ids[None, :], axis=0)
    token_mask = jnp.repeat(present.astype(jnp.float32), block_len)
    activations = hidden[0]
    projected = jnp.dot(activations, proj_weight, preferred_element_type=jnp.float32)
    decay_rate = -jnp.exp(log_rate)
    masked_step = step_size[0] * token_mask[None, :]
    values = scan_input[0].astype(jnp.float32).reshape(token_count, head_count, head_width)
    upstream = grad_out[0].astype(jnp.float32).reshape(token_count, head_count, head_width)
    log_steps = masked_step * decay_rate[:, None]
    total_decay = jnp.exp(jnp.sum(log_steps, axis=1))
    zero_state = jnp.zeros((head_count, head_width, state_width), jnp.float32)
    local_state = zero_state
    before = jnp.zeros((head_count,), jnp.float32)
    local_state = lax.cond(
        present[0],
        group_tail,
        keep_state,
        local_state,
        values,
        projected[0:block_len, :state_width],
        masked_step,
        decay_rate,
    )
    pulled = lax.cond(
        present[0],
        pull_group,
        empty_pull,
        before,
        projected[0:block_len, state_width:],
        upstream,
        log_steps,
    )
    incoming = zero_state
    outgoing_grad = zero_state
    incoming = from_behind(total_decay[:, None, None] * incoming + local_state, "seq", 1)
    outgoing_grad = from_behind(total_decay[:, None, None] * outgoing_grad + pulled, "seq", -1)

    def layer(values_in, projected_in, step_in, rate_in, gain_in, start_state):
        rate_now = -jnp.exp(rate_in)
        step_now = step_in * token_mask[None, :]
        carry_state = start_state
        carry_state, piece = lax.cond(
            present[0],
            group_forward,
            pass_group,
            carry_state,
            values_in,
            projected_in[0:block_len, :state_width],
            projected_in[0:block_len, state_width:],
            step_now,
            rate_now,
            gain_in,
        )
        pieces = [piece]
        return (jnp.concatenate(pieces, axis=0), carry_state)

    _, pullback = jax.vjp(layer, values, projected, step_size[0], log_rate, skip_gain, incoming)
    grad_values, grad_proj, grad_steps, grad_rates, grad_gains, _ = pullback(
        (upstream, outgoing_grad)
    )
    grad_w = jnp.dot(activations.astype(jnp.float32).T, grad_proj, precision=exact_mode)
    scenes = lax.axis_size("dp")
    summed_w, summed_rate, summed_gain = lax.psum((grad_w, grad_rates, grad_gains), ("seq", "dp"))
    position = lax.axis_index("seq")
    row_share = summed_w.shape[0] // lax.axis_size("seq")
    head_share = head_count // lax.axis_size("seq")
    summed_w = lax.dynamic_slice_in_dim(summed_w, position * row_share, row_share, 0)
    summed_rate = lax.dynamic_slice_in_dim(summed_rate, position * head_share, head_share, 0)
    summed_gain = lax.dynamic_slice_in_dim(summed_gain, position * head_share, head_share, 0)
    grad_input = grad_values.reshape(1, token_count, head_count * head_width).astype(jnp.bfloat16)
    return (
        grad_input,
        grad_steps[None],
        summed_w / scenes,
        summed_rate / scenes,
        summed_gain / scenes,
    )


def solution(mesh):
    in_specs = (
        P("dp", "seq", None),
        P("dp", "seq", None),
        P("dp", "seq", None),
        P("dp", None, "seq"),
        P(),
        P(),
        P(),
        P("dp", "seq"),
    )
    out_specs = (P("dp", "seq", None), P("dp", None, "seq"), P("seq", None), P("seq"), P("seq"))
    return jax.shard_map(shards, mesh=mesh, in_specs=in_specs, out_specs=out_specs, check_vma=False)
```

profile of v0, /device:TPU:4, one launch (start us, length us, event | category | flops | bytes accessed | tf_op | source)
XLA Modules:
  0.0 424.6 jit_solution(2022731106091471074)
XLA Ops:
  7.2 0.0 copy-start
  7.2 0.0 all-reduce.9.cloned.1.call-start
  8.0 0.7 exponential_negate_fusion
  8.6 0.0 copy-done
  8.6 1.8 fusion.46
  10.5 1.6 copy.93
  12.1 1.9 convert.4
  14.0 0.0 copy-start.18
  14.0 2.8 copy.95
  16.8 0.0 copy-done.18
  16.8 0.2 fusion.48
  17.0 0.2 conditional.4
  17.0 0.1 broadcast.97
  17.2 1.2 conditional.6
  17.2 1.2 broadcast.95
  18.4 0.0 copy-start.21
  18.4 2.6 broadcast_add_fusion
  21.1 2.8 collective-permute-start
  23.8 1.3 collective-permute-start.1
  25.1 0.4 collective-permute-done
  25.6 0.0 copy-done.21
  25.6 27.4 %conditional.5 = (f32[256,40,64]{2,1,0:T(8,128)}, f32[40,1]{0,1:T(1,128)S(1)}, f32[40,256]{1,0:T(8,128)S(1)}, pred[40,256,256]{2,1,0:T(32,128)(4,1)}, f32[40,256...) conditional(s32[]{:T(128)} %bitcast.29, () %tuple.51, ...), branch_computations={%region_9.10_spmd, %region_10.13_spmd} | conditional | flops 1119864960 | bytes 55766932 | solution.py:118
  25.6 5.2 %broadcast.104 = f32[40,256,256]{2,1,0:T(8,128)} broadcast(f32[]{:T(128)} %constant.25.clone), dimensions={} | broadcast | bytes 10485764 | tf_op jit(solution)/shard_map/broadcast.27
  30.8 5.1 %broadcast.104.clone = f32[40,256,256]{2,1,0:T(8,128)} broadcast(f32[]{:T(128)} %constant.25.clone), dimensions={} | broadcast | bytes 10485764 | tf_op jit(solution)/shard_map/broadcast.27
  35.9 5.2 %broadcast.104.clone.1 = f32[40,256,256]{2,1,0:T(8,128)} broadcast(f32[]{:T(128)} %constant.25.clone), dimensions={} | broadcast | bytes 10485764 | tf_op jit(solution)/shard_map/broadcast.27
  41.1 2.6 broadcast.100
  43.7 2.6 broadcast.100.clone.1
  46.3 1.8 broadcast.100.clone
  48.1 2.7 broadcast.103
  50.8 1.2 broadcast.108
  52.1 0.6 broadcast.102.clone
  52.9 0.0 collective-permute-done.1
  52.9 11.3 %conditional.7 = (f32[40,256]{1,0:T(8,128)}, f32[40]{0:T(128)}, f32[256,256]{1,0:T(8,128)}, f32[40]{0:T(128)}, bf16[1,256,2560]{2,1,0:T(8,128)(2,1)}) conditional(s32[]{:T(128)} %bitcast.29, () %tuple.50, (f32[256,128]{1,0:T(8,128)S(1)}, f32[40,64,128]{2,1,0:T(8,128)S(1)}, f32[256,40,64]{2,1,0:T(8,128)}, f32[40,256]{1,0:T(8,128)S(1)}, ...), branch_computations={%region_13.14_spmd, %region_14.27_spmd} | conditional | flops 7284011008 | bytes 102498304 | solution.py:118
  53.0 0.7 pad_add_fusion
  53.7 1.1 reshape.168.clone
  54.8 0.6 broadcast.113
  55.4 0.5 broadcast.114
  56.0 0.5 broadcast.120
  64.3 0.0 copy-start.22
  64.3 3.7 convolution_bitcast_fusion
  68.0 0.0 all-reduce.9.cloned.1.call-update
  68.0 0.0 copy-done.22
  68.0 0.6 exponential_multiply_fusion.2
  68.6 159.7 %all-reduce.6 = (f32[40]{0:T(128)S(1)}, f32[40]{0:T(128)S(1)}) all-reduce(f32[40]{0:T(128)S(1)} %exponential_multiply_fusion.2, f32[40]{0:T(128)} %get-tuple-element.204), channel_id=1, replica_groups=mesh['seq'=2,'dp'=128] {'seq','dp'}, use_global_device_ids=true, to_apply=%region_28.29 | all-reduce | flops 80 | bytes 640 | tf_op jit(solution)/shard_map/psum | solution.py:139
  228.3 0.6 dynamic-slice_multiply_fusion.1
  228.9 1.4 multiply_bitcast_fusion.6
  230.3 184.3 %all-reduce.9.cloned.1.call-done = f32[2560,256]{0,1:T(8,128)} async-done(((f32[2560,256]{0,1:T(8,128)}), f32[2560,256]{0,1:T(8,128)}) %all-reduce.9.cloned.1.call-update) | async-done | bytes 2621456 | tf_op jit(solution)/shard_map/psum | solution.py:139
  414.6 1.4 dynamic-slice_multiply_fusion
  416.0 1.5 copy.99
  (14 shorter events, 0.1 us)
Async XLA Ops:
  7.2 1.5 copy-start
  7.2 407.4 %all-reduce.9.cloned.1.call-start = ((), (), s32[]{:S(2)}) async-start(), calls=%async_computation | async-start | bytes 5242880 | tf_op jit(solution)/shard_map/psum | solution.py:139
  14.0 2.9 copy-start.18
  18.4 7.1 %copy-start.21 = (f32[40]{0:T(128)S(1)}, f32[40]{0:T(128)}, u32[]{:S(2)}) copy-start(f32[40]{0:T(128)} %param.22) | copy-start | bytes 484
  21.1 4.5 %collective-permute-start = (f32[40,64,128]{2,1,0:T(8,128)S(1)}, f32[40,64,128]{2,1,0:T(8,128)}, u32[]{:S(2)}, u32[]{:S(2)}) collective-permute-start(f32[40,64,128]{2,1,0:T(8,128)S(1)} %get-tuple-element.452), channel_id=1, source_target_pairs={{0,128},{1,129},{2,130},{3,131},{4,132},{5,133},{6,134},{7,135},{8... | collective-permute-start | bytes 3932168 | tf_op jit(solution)/shard_map/ppermute | solution.py:12
  23.8 29.1 %collective-permute-start.1 = (f32[40,64,128]{2,1,0:T(8,128)}, f32[40,64,128]{2,1,0:T(8,128)S(1)}, u32[]{:S(2)}, u32[]{:S(2)}) collective-permute-start(f32[40,64,128]{2,1,0:T(8,128)} %get-tuple-element.451), channel_id=1, source_target_pairs={{128,0},{129,1},{130,2},{131,3},{132,4},{133,5},{134,6},{135,7},{1... | collective-permute-start | bytes 3932168 | tf_op jit(solution)/shard_map/ppermute | solution.py:12
  64.3 3.8 copy-start.22
Sparse Core Ops, SparseCore 0:
  68.1 346.4 all-reduce.8
where the time goes:
time: 433 us; the launch traced here: 425 us
  waiting for transfers between devices  185 us (43%)
  blocking collectives  160 us (37%)
  local copies, waits for them, and re-layouts  37.2 us (9%)
  between operations  15.1 us (3%)
  other arithmetic  10.1 us (2%)
  loops' own time  8.11 us (2%)
  matrix products  5.54 us (1%)
    psum x1, waiting for transfers between devices, shards(): lax.psum((grad_w, grad_rates, grad_gains), ('seq', 'dp'))  184 us
    psum x1, blocking collectives, shards(): lax.psum((grad_w, grad_rates, grad_gains), ('seq', 'dp'))  160 us
    another operation x26, local copies, waits for them, and re-layouts  30.1 us
  transfers between devices with their start and end apart: 3, of which 2 were waited for; matrix products, arithmetic and copies ran while one was open for 7% of the time, Pallas kernels for 0%

commit v1 on v0

v1 whole, which is shorter than its diff:
```python
import jax
import jax.numpy as jnp
from jax import lax
from jax.experimental import pallas as pl
from jax.experimental.pallas import tpu as pltpu
from jax.sharding import PartitionSpec as P

F32 = jnp.float32
BF16 = jnp.bfloat16
HEADS = 40
WIDTH = 64
STATE = 128
TOK = 256
FEAT = HEADS * WIDTH
SCENES = 128
STEP_HEADS = 8
GROUPS = HEADS // STEP_HEADS
STEP_FEAT = STEP_HEADS * WIDTH
HALF = FEAT // 2
VMEM = 48 * 1024 * 1024

NN = (((1,), (0,)), ((), ()))
NT = (((1,), (1,)), ((), ()))
TN = (((0,), (0,)), ((), ()))


def dot(a, b, dims):
    return lax.dot_general(a, b, dims, preferred_element_type=F32)


def split2(v):
    high = v.astype(BF16)
    return high, (v - high.astype(F32)).astype(BF16)


def split3(v):
    rows = v.shape[0]
    high = v.astype(BF16).astype(F32)
    rest = v - high
    mid = rest.astype(BF16).astype(F32)
    low = rest - mid
    parts = [high, mid, low]
    extra = -3 * rows % 16
    if extra:
        parts.append(jnp.zeros((extra, v.shape[1]), F32))
    return jnp.concatenate(parts, axis=0).astype(BF16)


def dot3(a, b, dims):
    ah, al = split2(a)
    bh, bl = split2(b)
    return dot(ah, bh, dims) + dot(al, bh, dims) + dot(ah, bl, dims)


def head_rows(rows, heads, width):
    row = lax.broadcasted_iota(jnp.int32, (rows, width), 0)
    head = lax.broadcasted_iota(jnp.int32, (rows, width), 1) // WIDTH
    hit = (head == row) | (head == row - heads) | (head == row - 2 * heads)
    return jnp.where(hit & (row < 3 * heads), 1.0, 0.0)


def spread_heads(v, width):
    parts = split3(v)
    return dot(parts, head_rows(parts.shape[0], v.shape[0], width).astype(BF16), TN)


def sum_parts(v, heads):
    return v[:heads] + v[heads : 2 * heads] + v[2 * heads : 3 * heads]


def state_kernel(
    tile_ref, hidden_hbm, weight_hbm, x_hbm, g_hbm, step_ref, rate_ref,
    proj_ref, run_ref, cols_ref, scale_ref, high_ref, low_ref, send_ref,
    hidden, weight, values, sems,
):
    role = lax.axis_index("seq")
    copies = []
    for c in range(GROUPS):
        part = pl.ds(c * STEP_FEAT, STEP_FEAT)
        copies.append(pltpu.make_async_copy(hidden_hbm.at[:, part], hidden.at[:, part], sems.at[c]))
        copies.append(pltpu.make_async_copy(weight_hbm.at[part], weight.at[part], sems.at[GROUPS + c]))
    for copy in copies:
        copy.start()
    take_x = pltpu.make_async_copy(x_hbm, values, sems.at[2 * GROUPS])
    take_g = pltpu.make_async_copy(g_hbm, values, sems.at[2 * GROUPS])

    @pl.when(role == 0)
    def _():
        take_x.start()

    @pl.when(role != 0)
    def _():
        take_g.start()

    present = jnp.where(tile_ref[0, 0] == 0, 1.0, 0.0).astype(F32)
    step = step_ref[...]
    rate = -jnp.exp(rate_ref[...])
    logs = step * present * rate
    row = lax.broadcasted_iota(jnp.int32, (TOK, TOK), 0)
    col = lax.broadcasted_iota(jnp.int32, (TOK, TOK), 1)
    upto = jnp.where(row <= col, 1.0, 0.0).astype(BF16)
    run = sum_parts(dot(split3(logs), upto, NN), HEADS)
    run_ref[...] = run
    less = run - jnp.log(step)
    turned = jnp.concatenate([less, jnp.zeros((STATE - HEADS, TOK), F32)], axis=0).T
    for k in range(GROUPS):
        cols_ref[k] = turned[:, k * STEP_HEADS : (k + 1) * STEP_HEADS]
    tail = step * jnp.exp(run[:, TOK - 1 :] - run)
    scale = jnp.where(role == 0, tail, jnp.exp(run)) * present
    scale_ref[...] = scale

    proj = jnp.zeros((TOK, 2 * STATE), F32)
    for c in range(GROUPS):
        copies[2 * c].wait()
        copies[2 * c + 1].wait()
        part = slice(c * STEP_FEAT, (c + 1) * STEP_FEAT)
        proj = proj + dot(hidden[:, part], weight[part, :], NN)
    proj_ref[...] = proj
    mine = jnp.where(role == 0, proj[:, :STATE], proj[:, STATE:])
    mine_high, mine_low = split2(mine)
    take_x.wait()
    parts = split3(scale)
    for c in range(GROUPS):
        part = slice(c * STEP_FEAT, (c + 1) * STEP_FEAT)
        r = lax.broadcasted_iota(jnp.int32, (parts.shape[0], STEP_FEAT), 0)
        h = lax.broadcasted_iota(jnp.int32, (parts.shape[0], STEP_FEAT), 1) // WIDTH + c * STEP_HEADS
        hit = (h == r) | (h == r - HEADS) | (h == r - 2 * HEADS)
        pick = jnp.where(hit, 1.0, 0.0).astype(BF16)
        scaled = dot(parts, pick, TN) * values[:, part].astype(F32)
        high, low = split2(scaled)
        high_ref[:, part] = high
        low_ref[:, part] = low
        send_ref[:, part] = dot(mine_high, high, TN) + dot(mine_low, high, TN) + dot(mine_high, low, TN)


def state_call(tile, hidden, weight, x, g, step, log_rate):
    vm = pl.BlockSpec(memory_space=pltpu.VMEM)
    hbm = pl.BlockSpec(memory_space=pl.ANY)
    return pl.pallas_call(
        state_kernel,
        name="state_to_send",
        out_shape=(
            jax.ShapeDtypeStruct((TOK, 2 * STATE), F32),
            jax.ShapeDtypeStruct((HEADS, TOK), F32),
            jax.ShapeDtypeStruct((GROUPS, TOK, STEP_HEADS), F32),
            jax.ShapeDtypeStruct((HEADS, TOK), F32),
            jax.ShapeDtypeStruct((TOK, FEAT), BF16),
            jax.ShapeDtypeStruct((TOK, FEAT), BF16),
            jax.ShapeDtypeStruct((STATE, FEAT), F32),
        ),
        in_specs=[pl.BlockSpec(memory_space=pltpu.SMEM), hbm, hbm, hbm, hbm, vm, vm],
        out_specs=(vm,) * 7,
        scratch_shapes=[
            pltpu.VMEM((TOK, FEAT), BF16),
            pltpu.VMEM((FEAT, 2 * STATE), BF16),
            pltpu.VMEM((TOK, FEAT), BF16),
            pltpu.SemaphoreType.DMA((2 * GROUPS + 1,)),
        ],
        compiler_params=pltpu.CompilerParams(vmem_limit_bytes=VMEM),
        cost_estimate=pl.CostEstimate(flops=1_000_000_000, bytes_accessed=8_000_000, transcendentals=20_000),
    )(tile, hidden, weight, x, g, step, log_rate)


def causal_bias():
    row = lax.broadcasted_iota(jnp.int32, (STATE, STATE), 0)
    col = lax.broadcasted_iota(jnp.int32, (STATE, STATE), 1)
    return jnp.where(col >= row, 0.0, -1e30).astype(F32)


def own_half(v, which):
    lane = lax.broadcasted_iota(jnp.int32, v.shape, 1)
    keep = (lane < WIDTH) if which == 0 else (lane >= WIDTH)
    return jnp.where(keep, v, jnp.zeros_like(v))


def decays(run_row, less_col, bias):
    d = run_row - less_col
    first = jnp.exp(jnp.concatenate([d[:STATE, :STATE] + bias, d[:STATE, STATE:]], axis=1))
    second = jnp.exp(d[STATE:, STATE:] + bias)
    return first, second


def pair_kernel(x_ref, g_ref, run_ref, cols_ref, out_ref):
    bias = causal_bias()
    first = jnp.zeros((STATE, TOK), F32)
    second = jnp.zeros((STATE, STATE), F32)
    for r in range(STEP_HEADS):
        lanes = slice(r // 2 * 128, r // 2 * 128 + 128)
        x = x_ref[:, lanes]
        g = own_half(g_ref[:, lanes], r % 2)
        d1, d2 = decays(run_ref[r : r + 1, :], cols_ref[0][:, r : r + 1], bias)
        first = first + d1 * dot(x[:STATE], g, NT)
        second = second + d2 * dot(x[STATE:], g[STATE:], NT)

    @pl.when(pl.program_id(0) == 0)
    def _():
        out_ref[...] = jnp.zeros_like(out_ref)

    out_ref[:STATE, :] += first
    out_ref[STATE:, STATE:] += second


def pair_call(x, g, run, cols):
    return pl.pallas_call(
        pair_kernel,
        name="score_gradient",
        grid=(GROUPS,),
        out_shape=jax.ShapeDtypeStruct((TOK, TOK), F32),
        in_specs=[
            pl.BlockSpec((TOK, STEP_FEAT), lambda k: (0, k)),
            pl.BlockSpec((TOK, STEP_FEAT), lambda k: (0, k)),
            pl.BlockSpec((STEP_HEADS, TOK), lambda k: (k, 0)),
            pl.BlockSpec((1, TOK, STEP_HEADS), lambda k: (k, 0, 0)),
        ],
        out_specs=pl.BlockSpec((TOK, TOK), lambda k: (0, 0)),
        compiler_params=pltpu.CompilerParams(vmem_limit_bytes=VMEM),
        cost_estimate=pl.CostEstimate(flops=1_500_000_000, bytes_accessed=3_000_000, transcendentals=2_600_000),
    )(x, g, run, cols)


def weight_kernel(
    tile_ref, pair_ref, proj_ref, high_ref, low_ref, state_ref, hidden_ref, keep_ref, send_ref
):
    role = lax.axis_index("seq")
    present = jnp.where(tile_ref[0, 0] == 0, 1.0, 0.0).astype(F32)
    pair = pair_ref[...] * present
    proj = proj_ref[...]
    keys = dot3(pair, proj[:, STATE:], NN)
    query = dot3(pair, proj[:, :STATE], TN)
    both = jnp.concatenate(split2(state_ref[...]), axis=0)
    high = dot(high_ref[...], both, NT)
    across = high[:, :STATE] + high[:, STATE:] + dot(low_ref[...], both[:STATE], NT)
    keys = keys + jnp.where(role == 0, across, 0.0)
    query = query + jnp.where(role == 0, 0.0, across)
    grad = jnp.concatenate([keys, query], axis=1) * (1.0 / SCENES)
    terms = jnp.concatenate(split2(grad), axis=1)
    chunk = 256
    for out_ref, base in ((send_ref, (1 - role) * HALF), (keep_ref, role * HALF)):
        for c in range(HALF // chunk):
            lanes = pl.ds(pl.multiple_of(base + c * chunk, 128), chunk)
            got = dot(hidden_ref[:, lanes], terms, TN)
            out_ref[c * chunk : (c + 1) * chunk, :] = got[:, : 2 * STATE] + got[:, 2 * STATE :]


def weight_call(tile, pair, proj, high, low, state, hidden):
    vm = pl.BlockSpec(memory_space=pltpu.VMEM)
    return pl.pallas_call(
        weight_kernel,
        name="weight_gradient",
        out_shape=(
            jax.ShapeDtypeStruct((HALF, 2 * STATE), F32),
            jax.ShapeDtypeStruct((HALF, 2 * STATE), F32),
        ),
        in_specs=[pl.BlockSpec(memory_space=pltpu.SMEM)] + [vm] * 6,
        out_specs=(vm, vm),
        compiler_params=pltpu.CompilerParams(vmem_limit_bytes=VMEM),
        cost_estimate=pl.CostEstimate(flops=1_500_000_000, bytes_accessed=8_000_000, transcendentals=0),
    )(tile, pair, proj, high, low, state, hidden)


def input_kernel(
    tile_ref, x_ref, g_ref, run_ref, cols_ref, scale_ref, step_ref, rate_ref, gain_ref, state_ref, proj_ref,
    dx_ref, dstep_ref, small_ref,
    scores, rows,
):
    role = lax.axis_index("seq")
    first_role = jnp.where(role == 0, 1.0, 0.0).astype(F32)
    present = jnp.where(tile_ref[0, 0] == 0, 1.0, 0.0).astype(F32)
    k = pl.program_id(0)

    @pl.when(k == 0)
    def _():
        small_ref[...] = jnp.zeros_like(small_ref)
        scores[...] = dot3(proj_ref[:, :STATE], proj_ref[:, STATE:], NT) * present

    bias = causal_bias()
    state = state_ref[...]
    mine = jnp.where(role == 0, proj_ref[:, :STATE], proj_ref[:, STATE:])
    carried = spread_heads(scale_ref[...], STEP_FEAT) * dot3(mine, state, NN)
    select = head_rows(STEP_HEADS, STEP_HEADS, STEP_FEAT)
    gain_row = jnp.sum(select * gain_ref[...], axis=0, keepdims=True) * present
    x_all = x_ref[...].astype(F32)
    g_all = g_ref[...].astype(F32)
    within = []
    for q in range(STEP_HEADS // 2):
        lanes = slice(q * 128, q * 128 + 128)
        x = x_ref[:, lanes]
        upper = jnp.zeros((STATE, 128), F32)
        lower = jnp.zeros((STATE, 128), F32)
        for half in range(2):
            r = 2 * q + half
            g = own_half(g_ref[:, lanes], half)
            d1, d2 = decays(run_ref[r : r + 1, :], cols_ref[0][:, r : r + 1], bias)
            m1 = d1 * scores[:STATE, :]
            m2 = d2 * scores[STATE:, STATE:]
            f1 = jnp.sum(m1 * dot(x[:STATE], g, NT), axis=0, keepdims=True)
            f2 = jnp.sum(m2 * dot(x[STATE:], g[STATE:], NT), axis=0, keepdims=True)
            rows[r : r + 1, :STATE] = f1[:, :STATE]
            rows[r : r + 1, STATE:] = f1[:, STATE:] + f2
            h1, l1 = split2(m1)
            h2, l2 = split2(m2)
            upper = upper + dot(h1, g, NN) + dot(l1, g, NN)
            lower = lower + dot(h2, g[STATE:], NN) + dot(l2, g[STATE:], NN)
        within.append(jnp.concatenate([upper, lower], axis=0))
    total = jnp.concatenate(within, axis=1) + first_role * carried
    dx_ref[...] = (total + gain_row * g_all).astype(BF16)

    own = jnp.where(role == 0, x_all, g_all)
    pick = jnp.concatenate([select, jnp.zeros_like(select)], axis=0).astype(BF16)
    by_x_high, by_x_low = split2(x_all * total)
    by_x = (dot(pick, by_x_high, NT) + dot(pick, by_x_low, NT))[:STEP_HEADS]
    by_own_high, by_own_low = split2(own * carried)
    by_own = (dot(pick, by_own_high, NT) + dot(pick, by_own_low, NT))[:STEP_HEADS]
    slope = rows[...] - by_x + (1.0 - first_role) * by_own
    row = lax.broadcasted_iota(jnp.int32, (TOK, TOK), 0)
    col = lax.broadcasted_iota(jnp.int32, (TOK, TOK), 1)
    after = jnp.where(row >= col, 1.0, 0.0).astype(BF16)
    logs = sum_parts(dot(split3(slope), after, NN), STEP_HEADS)
    logs = logs + first_role * jnp.sum(by_own, axis=1, keepdims=True)
    step = step_ref[...]
    rate = -jnp.exp(rate_ref[...])
    dstep_ref[...] = by_x / step + rate * logs
    d_rate = rate * present * jnp.sum(step * logs, axis=1, keepdims=True)
    gx = jnp.sum(g_all * x_all, axis=0, keepdims=True) * present
    d_gain = jnp.sum(select * gx, axis=1, keepdims=True)
    r8 = lax.broadcasted_iota(jnp.int32, (8, 128), 0)
    lane = lax.broadcasted_iota(jnp.int32, (8, 128), 1)
    spot = lane == r8 + k * STEP_HEADS
    small_ref[:, :128] += jnp.where(spot, d_rate * (1.0 / SCENES), 0.0)
    small_ref[:, 128:] += jnp.where(spot, d_gain * (1.0 / SCENES), 0.0)


def input_call(tile, x, g, run, cols, scale, step, log_rate, gain, state, proj):
    feat = pl.BlockSpec((TOK, STEP_FEAT), lambda k: (0, k))
    head = pl.BlockSpec((STEP_HEADS, TOK), lambda k: (k, 0))
    one = pl.BlockSpec((STEP_HEADS, 1), lambda k: (k, 0))
    return pl.pallas_call(
        input_kernel,
        name="input_gradient",
        grid=(GROUPS,),
        out_shape=(
            jax.ShapeDtypeStruct((TOK, FEAT), BF16),
            jax.ShapeDtypeStruct((HEADS, TOK), F32),
            jax.ShapeDtypeStruct((8, 256), F32),
        ),
        in_specs=[
            pl.BlockSpec(memory_space=pltpu.SMEM),
            feat,
            feat,
            head,
            pl.BlockSpec((1, TOK, STEP_HEADS), lambda k: (k, 0, 0)),
            head,
            head,
            one,
            one,
            pl.BlockSpec((STATE, STEP_FEAT), lambda k: (0, k)),
            pl.BlockSpec((TOK, 2 * STATE), lambda k: (0, 0)),
        ],
        out_specs=(feat, head, pl.BlockSpec((8, 256), lambda k: (0, 0))),
        scratch_shapes=[pltpu.VMEM((TOK, TOK), F32), pltpu.VMEM((STEP_HEADS, TOK), F32)],
        compiler_params=pltpu.CompilerParams(vmem_limit_bytes=VMEM),
        cost_estimate=pl.CostEstimate(flops=6_000_000_000, bytes_accessed=8_000_000, transcendentals=2_600_000),
    )(tile, x, g, run, cols, scale, step, log_rate, gain, state, proj)


SIZES = {"z": 8, "y": 4, "x": 4}
STRIDE = {"z": 16, "y": 4, "x": 1}


def moved(axis, new):
    n, s = SIZES[axis], STRIDE[axis]
    pairs = []
    for i in range(SCENES):
        c = i // s % n
        pairs.append((i, i + (new(c) - c) * s))
    return pairs


def shift(v, axis, k):
    return lax.ppermute(v, "dp", moved(axis, lambda c: (c + k) % SIZES[axis]))


def scatter_sum(v, axis, extra=None):
    n = SIZES[axis]
    r = v.shape[0] // n
    me = lax.axis_index("dp") // STRIDE[axis] % n
    total = lax.dynamic_slice_in_dim(v, me * r, r, 0)
    if extra is not None:
        total = jnp.concatenate([total, extra], axis=0)
    for k in range(1, n):
        piece = lax.dynamic_slice_in_dim(v, lax.rem(me + k, n) * r, r, 0)
        if extra is not None:
            piece = jnp.concatenate([piece, extra], axis=0)
        total = total + shift(piece, axis, k)
    return total


def gather(v, axis):
    n = SIZES[axis]
    me = lax.axis_index("dp") // STRIDE[axis] % n
    return me, [v] + [shift(v, axis, k) for k in range(1, n)]


def laid(me, pieces, r):
    n = len(pieces)
    out = jnp.zeros((n * r, pieces[0].shape[1]), F32)
    for k, piece in enumerate(pieces):
        out = lax.dynamic_update_slice_in_dim(out, piece[:r], lax.rem(me + n - k, n) * r, 0)
    return out


def swap(v):
    return lax.ppermute(v, "seq", [(0, 1), (1, 0)])


def shards(hidden, scan_input, grad_out, step_size, proj_weight, log_rate, skip_gain, tile_list):
    role = lax.axis_index("seq")
    hid, x, g, step = hidden[0], scan_input[0], grad_out[0], step_size[0]
    rate_col = log_rate[:, None]
    gain_col = skip_gain[:, None]
    proj, run, cols, scale, high, low, send = state_call(tile_list, hid, proj_weight, x, g, step, rate_col)
    state = swap(send)
    pair = pair_call(x, g, run, cols)
    keep, give = weight_call(tile_list, pair, proj, high, low, state, hid)
    half = keep + swap(give)
    dx, dstep, small = input_call(
        tile_list, x, g, run, cols, scale, step, rate_col, gain_col, state, proj
    )
    part = scatter_sum(half, "x")
    small = small + swap(small)
    part = scatter_sum(part, "y", small)
    for d in (1, 2, 4):
        part = part + lax.ppermute(part, "dp", moved("z", lambda c, d=d: c ^ d))
    rows = HALF // 16
    me, pieces = gather(part[:rows], "y")
    wide = jnp.concatenate([laid(me, pieces, rows), part[rows:]], axis=0)
    me, pieces = gather(wide, "x")
    grad_weight = laid(me, pieces, rows * 4)
    small = sum(piece[rows * 4 :] for piece in pieces)
    small = jnp.sum(small, axis=0)
    share = HEADS // 2
    d_rate = lax.dynamic_slice_in_dim(small[:HEADS], role * share, share, 0)
    d_gain = lax.dynamic_slice_in_dim(small[128 : 128 + HEADS], role * share, share, 0)
    return dx[None], dstep[None], grad_weight, d_rate, d_gain


def solution(mesh):
    in_specs = (
        P("dp", "seq", None),
        P("dp", "seq", None),
        P("dp", "seq", None),
        P("dp", None, "seq"),
        P(),
        P(),
        P(),
        P("dp", "seq"),
    )
    out_specs = (P("dp", "seq", None), P("dp", None, "seq"), P("seq", None), P("seq"), P("seq"))
    return jax.shard_map(shards, mesh=mesh, in_specs=in_specs, out_specs=out_specs, check_vma=False)
```

time: 433 us -> 99.3 us (0.23)
  the two profiles are of different devices: /device:TPU:4 before, /device:TPU:6 now
where the time goes in v1:
time: 99.3 us; the launch traced here: 99.1 us
  waiting for transfers between devices  39.4 us (40%)
  starting transfers between devices  24.6 us (25%)
  Pallas kernels  22.9 us (23%)
  local copies, waits for them, and re-layouts  7.29 us (7%)
  other arithmetic  3.34 us (3%)
  between operations  1.58 us (2%)
    ppermute x12, waiting for transfers between devices, shift(): return lax.ppermute(v, 'dp', moved(axis, lambda c: (c + k) % SIZES[axis]))  24.7 us
    ppermute x12, starting transfers between devices, shift(): return lax.ppermute(v, 'dp', moved(axis, lambda c: (c + k) % SIZES[axis]))  14.4 us
    pallas_call x1, Pallas kernels, input_call(): pl.pallas_call(input_kernel, name='input_gradient', grid=(GROUPS,), out_s...  11 us
    ppermute x3, waiting for transfers between devices, shards(): part = part + lax.ppermute(part, 'dp', moved('z', lambda c, d=d: c ^ d))  10.6 us
    ppermute x3, starting transfers between devices, shards(): part = part + lax.ppermute(part, 'dp', moved('z', lambda c, d=d: c ^ d))  9.67 us
    pallas_call x1, Pallas kernels, state_call(): pl.pallas_call(state_kernel, name='state_to_send', out_shape=(jax.ShapeDt...  4.53 us
    pallas_call x1, Pallas kernels, weight_call(): pl.pallas_call(weight_kernel, name='weight_gradient', out_shape=(jax.Shap...  4.4 us
    ppermute x3, waiting for transfers between devices, swap(): return lax.ppermute(v, 'seq', [(0, 1), (1, 0)])  4.06 us
  transfers between devices with their start and end apart: 18, of which 16 were waited for; matrix products, arithmetic and copies ran while one was open for 0% of the time, Pallas kernels for 14%

profile of v1, /device:TPU:6, one launch (start us, length us, event | category | flops | bytes accessed | tf_op | source)
XLA Modules:
  0.0 99.1 jit_solution(10410029953716557458)
XLA Ops:
  1.3 0.7 copy.13.rate_ref
  2.0 0.8 copy-done.5
  2.8 4.5 %state_to_send.1 = (f32[256,256]{1,0:T(8,128)S(1)}, f32[40,256]{1,0:T(8,128)S(1)}, f32[5,256,8]{2,1,0:T(8,128)S(1)}, f32[40,256]{1,0:T(8,128)S(1)}, bf16[256,256...) custom-call(s32[1,1]{1,0:T(1,128)S(6)} %copy.24.tile_ref, bf16[256,2560]{1,0:T(8,128)(2,1)} %bitcast.16, ...), custom_call_target="tpu_custom_call" | custom-call | flops 1000000000 | bytes 8000000 | tf_op jit(solution)/shard_map/state_to_send/pallas_call | solution.py:139
  7.3 0.0 copy-start.7
  7.4 0.1 collective-permute-start
  7.5 0.0 copy-done
  7.5 0.0 copy-done.1
  7.5 2.9 %score_gradient.1.pair_ref = f32[256,256]{1,0:T(8,128)S(1)} custom-call(bf16[256,2560]{1,0:T(8,128)(2,1)S(1)} %bitcast.9, bf16[256,2560]{1,0:T(8,128)(2,1)S(1)} %bitcast.12, f32[40,256]{1,0:T(8,128)S(1)} %get-tuple-element.17.run_ref, f32[5,256,8]{2,1,0:T(8,128)S(1)} %get-tuple-element.18.cols_ref), custom_call_target="tpu_custom_call" | custom-call | flops 1500000000 | bytes 3000000 | tf_op jit(solution)/shard_map/score_gradient/pallas_call | solution.py:204
  10.4 0.0 copy-done.7
  10.4 0.1 collective-permute-done.state_ref
  10.5 1.1 %copy-done.2 = f32[128,2560]{1,0:T(8,128)} copy-done((f32[128,2560]{1,0:T(8,128)}, f32[128,2560]{1,0:T(8,128)S(1)}, u32[]{:S(2)}) %copy-start.2) | copy-done | bytes 1310744
  11.5 4.4 %weight_gradient.1 = (f32[1280,256]{1,0:T(8,128)S(1)}, f32[1280,256]{1,0:T(8,128)}) custom-call(s32[1,1]{1,0:T(1,128)S(6)} %copy.24.tile_ref, f32[256,256]{1,0:T(8,128)S(1)} %score_gradient.1.pair_ref, f32[256,256]{1,0:T(8,128)S(1)} %get-tuple-element.21.proj_ref, bf16[256,2560]{1,0:T(8,128)(2,1)S(1)} %get-tuple-element.24.high_ref, ...), custom_call_target="tpu_custom_call" | custom-call | flops 1500000000 | bytes 8000000 | tf_op jit(solution)/shard_map/weight_gradient/pallas_call | solution.py:247
  15.9 1.1 %copy-done.4 = f32[1280,256]{1,0:T(8,128)} copy-done((f32[1280,256]{1,0:T(8,128)}, f32[1280,256]{1,0:T(8,128)S(1)}, u32[]{:S(2)}) %copy-start.4) | copy-done | bytes 1310744
  17.0 0.4 collective-permute-start.1
  17.4 0.0 copy-done.11
  17.4 0.1 copy.15.gain_ref
  17.5 2.9 %collective-permute-done.1 = f32[1280,256]{1,0:T(8,128)} collective-permute-done((f32[1280,256]{1,0:T(8,128)}, f32[1280,256]{1,0:T(8,128)}, u32[]{:S(2)}, u32[]{:S(2)}) %collective-permute-start.1) | collective-permute-done | bytes 1310752 | tf_op jit(solution)/shard_map/ppermute | solution.py:413
  20.4 1.9 %add.141 = f32[1280,256]{1,0:T(8,128)S(1)} add(f32[1280,256]{1,0:T(8,128)} %copy-done.4, f32[1280,256]{1,0:T(8,128)} %collective-permute-done.1) | non-fusion elementwise | flops 327680 | bytes 3932160 | tf_op jit(solution)/shard_map/add | solution.py:425
  22.4 0.0 copy-start.9
  22.4 0.0 copy-start.3
  22.4 0.0 copy-start.6
  22.4 1.0 %constant_dynamic-slice_fusion.6 = (f32[320,256]{1,0:T(8,128)}, f32[320,256]{1,0:T(8,128)}, f32[320,256]{1,0:T(8,128)}) fusion(f32[1280,256]{1,0:T(8,128)S(1)} %add.141, s32[]{:T(128)S(6)} %select_n.64, s32[]{:T(128)S(6)} %select_n.66, s32[]{:T(128)S(6)} %select_n.65), kind=kLoop, calls=%fused_computation.27 | loop fusion | bytes 1966092 | tf_op jit(solution)/shard_map/dynamic_slice | solution.py:391
  23.4 2.2 %collective-permute-start.2 = (f32[320,256]{1,0:T(8,128)}, f32[320,256]{1,0:T(8,128)S(1)}, u32[]{:S(2)}, u32[]{:S(2)}) collective-permute-start(f32[320,256]{1,0:T(8,128)} %get-tuple-element.29), channel_id=1, source_target_pairs={{0,1},{1,2},{2,3},{3,0},{4,5},{5,6},{6,7},{7,4},{8,9},{9,10},{10,1... | collective-permute-start | bytes 983048 | tf_op jit(solution)/shard_map/ppermute | solution.py:380
  25.6 0.7 collective-permute-start.3
  26.3 0.2 collective-permute-start.4
  26.5 0.0 copy-done.8
  26.5 0.0 copy-done.3
  26.5 11.0 %input_gradient.1 = (bf16[256,2560]{1,0:T(8,128)(2,1)}, f32[40,256]{1,0:T(8,128)}, f32[8,256]{1,0:T(8,128)S(1)}) custom-call(s32[1,1]{1,0:T(1,128)S(6)} %copy.24.tile_ref, bf16[256,2560]{1,0:T(8,128)(2,1)S(1)} %bitcast.10, bf16[256,2560]{1,0:T(8,128)(2,1)S(1)} %bitcast.13, f32[40,256]{1,0:T(8,128)S(1)} %get-tuple-element.17.run_ref, ...), custom_call_target="tpu_custom_call" | custom-call | flops 6000000000 | bytes 8000000 | tf_op jit(solution)/shard_map/input_gradient/pallas_call | solution.py:337
  37.5 0.0 copy-done.9
  37.5 0.0 collective-permute-start.5
  37.6 1.1 %collective-permute-done.5 = f32[8,256]{1,0:T(8,128)S(1)} collective-permute-done((f32[8,256]{1,0:T(8,128)S(1)}, f32[8,256]{1,0:T(8,128)S(1)}, u32[]{:S(2)}, u32[]{:S(2)}) %collective-permute-start.5) | collective-permute-done | bytes 8224 | tf_op jit(solution)/shard_map/ppermute | solution.py:413
  38.7 1.8 %collective-permute-done.2 = f32[320,256]{1,0:T(8,128)S(1)} collective-permute-done((f32[320,256]{1,0:T(8,128)}, f32[320,256]{1,0:T(8,128)S(1)}, u32[]{:S(2)}, u32[]{:S(2)}) %collective-permute-start.2) | collective-permute-done | bytes 327712 | tf_op jit(solution)/shard_map/ppermute | solution.py:380
  40.5 0.0 collective-permute-done.3
  40.5 3.7 %collective-permute-done.4 = f32[320,256]{1,0:T(8,128)} collective-permute-done((f32[320,256]{1,0:T(8,128)}, f32[320,256]{1,0:T(8,128)}, u32[]{:S(2)}, u32[]{:S(2)}) %collective-permute-start.4) | collective-permute-done | bytes 327712 | tf_op jit(solution)/shard_map/ppermute | solution.py:380
  44.2 1.3 %add_add_fusion = f32[320,256]{1,0:T(8,128)S(1)} fusion(f32[320,256]{1,0:T(8,128)} %collective-permute-done.4, f32[320,256]{1,0:T(8,128)} %collective-permute-done.3, f32[320,256]{1,0:T(8,128)S(1)} %collective-permute-done.2, f32[1280,256]{1,0:T(8,128)} %copy-done.9, s32[]{:T(128)S(6)} %select_n.63), kind=kLoop, calls=%fused_computation.4 | loop fusion | flops 245760 | bytes 1638404 | tf_op jit(solution)/shard_map/add | solution.py:394
  45.5 0.1 collective-permute-start.6
  45.6 2.7 %collective-permute-start.7 = (f32[88,256]{1,0:T(8,128)S(1)}, f32[88,256]{1,0:T(8,128)S(1)}, u32[]{:S(2)}, u32[]{:S(2)}) collective-permute-start(f32[88,256]{1,0:T(8,128)S(1)} %get-tuple-element.39), channel_id=1, source_target_pairs={{0,8},{1,9},{2,10},{3,11},{4,12},{5,13},{6,14},{7,15},{8,0},{9,1},... | collective-permute-start | bytes 270344 | tf_op jit(solution)/shard_map/ppermute | solution.py:380
  48.3 1.3 %collective-permute-start.8 = (f32[88,256]{1,0:T(8,128)S(1)}, f32[88,256]{1,0:T(8,128)S(1)}, u32[]{:S(2)}, u32[]{:S(2)}) collective-permute-start(f32[88,256]{1,0:T(8,128)S(1)} %get-tuple-element.40), channel_id=1, source_target_pairs={{0,12},{1,13},{2,14},{3,15},{4,0},{5,1},{6,2},{7,3},{8,4},{9,5},{1... | collective-permute-start | bytes 270344 | tf_op jit(solution)/shard_map/ppermute | solution.py:380
  49.7 3.6 %collective-permute-done.6 = f32[88,256]{1,0:T(8,128)S(1)} collective-permute-done((f32[88,256]{1,0:T(8,128)S(1)}, f32[88,256]{1,0:T(8,128)S(1)}, u32[]{:S(2)}, u32[]{:S(2)}) %collective-permute-start.6) | collective-permute-done | bytes 90144 | tf_op jit(solution)/shard_map/ppermute | solution.py:380
  53.3 0.0 collective-permute-done.7
  53.3 0.6 collective-permute-done.8
  53.9 1.0 %collective-permute-start.9 = (f32[88,256]{1,0:T(8,128)S(1)}, f32[88,256]{1,0:T(8,128)S(1)}, u32[]{:S(2)}, u32[]{:S(2)}) collective-permute-start(f32[88,256]{1,0:T(8,128)S(1)} %fusion.2), channel_id=1, source_target_pairs={{0,16},{1,17},{2,18},{3,19},{4,20},{5,21},{6,22},{7,23},{8,24},{9,... | collective-permute-start | bytes 270344 | tf_op jit(solution)/shard_map/ppermute | solution.py:433
  54.9 3.6 %collective-permute-done.9 = f32[88,256]{1,0:T(8,128)S(1)} collective-permute-done((f32[88,256]{1,0:T(8,128)S(1)}, f32[88,256]{1,0:T(8,128)S(1)}, u32[]{:S(2)}, u32[]{:S(2)}) %collective-permute-start.9) | collective-permute-done | bytes 90144 | tf_op jit(solution)/shard_map/ppermute | solution.py:433
  58.5 2.4 %collective-permute-start.10 = (f32[88,256]{1,0:T(8,128)S(1)}, f32[88,256]{1,0:T(8,128)S(1)}, u32[]{:S(2)}, u32[]{:S(2)}) collective-permute-start(f32[88,256]{1,0:T(8,128)S(1)} %add.165), channel_id=1, source_target_pairs={{0,32},{1,33},{2,34},{3,35},{4,36},{5,37},{6,38},{7,39},{8,40},{9,... | collective-permute-start | bytes 270344 | tf_op jit(solution)/shard_map/ppermute | solution.py:433
  60.9 4.1 %collective-permute-done.10 = f32[88,256]{1,0:T(8,128)S(1)} collective-permute-done((f32[88,256]{1,0:T(8,128)S(1)}, f32[88,256]{1,0:T(8,128)S(1)}, u32[]{:S(2)}, u32[]{:S(2)}) %collective-permute-start.10) | collective-permute-done | bytes 90144 | tf_op jit(solution)/shard_map/ppermute | solution.py:433
  65.0 6.3 %collective-permute-start.11 = (f32[88,256]{1,0:T(8,128)S(1)}, f32[88,256]{1,0:T(8,128)S(1)}, u32[]{:S(2)}, u32[]{:S(2)}) collective-permute-start(f32[88,256]{1,0:T(8,128)S(1)} %add.166), channel_id=1, source_target_pairs={{0,64},{1,65},{2,66},{3,67},{4,68},{5,69},{6,70},{7,71},{8,72},{9,... | collective-permute-start | bytes 270344 | tf_op jit(solution)/shard_map/ppermute | solution.py:433
  71.3 2.9 %collective-permute-done.11 = f32[88,256]{1,0:T(8,128)S(1)} collective-permute-done((f32[88,256]{1,0:T(8,128)S(1)}, f32[88,256]{1,0:T(8,128)S(1)}, u32[]{:S(2)}, u32[]{:S(2)}) %collective-permute-start.11) | collective-permute-done | bytes 90144 | tf_op jit(solution)/shard_map/ppermute | solution.py:433
  74.3 1.8 %collective-permute-start.12 = (f32[80,256]{1,0:T(8,128)S(1)}, f32[80,256]{1,0:T(8,128)S(1)}, u32[]{:S(2)}, u32[]{:S(2)}) collective-permute-start(f32[80,256]{1,0:T(8,128)S(1)} %get-tuple-element.36), channel_id=1, source_target_pairs={{0,4},{1,5},{2,6},{3,7},{4,8},{5,9},{6,10},{7,11},{8,12},{9,13},{1... | collective-permute-start | bytes 245768 | tf_op jit(solution)/shard_map/ppermute | solution.py:380
  76.1 2.9 %collective-permute-start.13 = (f32[80,256]{1,0:T(8,128)S(1)}, f32[80,256]{1,0:T(8,128)S(1)}, u32[]{:S(2)}, u32[]{:S(2)}) collective-permute-start(f32[80,256]{1,0:T(8,128)S(1)} %get-tuple-element.36), channel_id=1, source_target_pairs={{0,8},{1,9},{2,10},{3,11},{4,12},{5,13},{6,14},{7,15},{8,0},{9,1},... | collective-permute-start | bytes 245768 | tf_op jit(solution)/shard_map/ppermute | solution.py:380
  78.9 0.3 collective-permute-start.14
  79.2 0.8 collective-permute-done.12
  80.0 2.2 %collective-permute-done.13 = f32[80,256]{1,0:T(8,128)S(1)} collective-permute-done((f32[80,256]{1,0:T(8,128)S(1)}, f32[80,256]{1,0:T(8,128)S(1)}, u32[]{:S(2)}, u32[]{:S(2)}) %collective-permute-start.13) | collective-permute-done | bytes 81952 | tf_op jit(solution)/shard_map/ppermute | solution.py:380
  82.2 1.1 %collective-permute-done.14 = f32[80,256]{1,0:T(8,128)S(1)} collective-permute-done((f32[80,256]{1,0:T(8,128)S(1)}, f32[80,256]{1,0:T(8,128)S(1)}, u32[]{:S(2)}, u32[]{:S(2)}) %collective-permute-start.14) | collective-permute-done | bytes 81952 | tf_op jit(solution)/shard_map/ppermute | solution.py:380
  83.4 1.1 %collective-permute-start.15 = (f32[328,256]{1,0:T(8,128)S(1)}, f32[328,256]{1,0:T(8,128)S(1)}, u32[]{:S(2)}, u32[]{:S(2)}) collective-permute-start(f32[328,256]{1,0:T(8,128)S(1)} %pad_maximum_fusion), channel_id=1, source_target_pairs={{0,1},{1,2},{2,3},{3,0},{4,5},{5,6},{6,7},{7,4},{8,9},{9,10},{10,1... | collective-permute-start | bytes 1007624 | tf_op jit(solution)/shard_map/ppermute | solution.py:380
  84.5 1.1 %collective-permute-start.16 = (f32[328,256]{1,0:T(8,128)S(1)}, f32[328,256]{1,0:T(8,128)S(1)}, u32[]{:S(2)}, u32[]{:S(2)}) collective-permute-start(f32[328,256]{1,0:T(8,128)S(1)} %pad_maximum_fusion), channel_id=1, source_target_pairs={{0,2},{1,3},{2,0},{3,1},{4,6},{5,7},{6,4},{7,5},{8,10},{9,11},{10,... | collective-permute-start | bytes 1007624 | tf_op jit(solution)/shard_map/ppermute | solution.py:380
  85.6 0.1 collective-permute-start.17
  85.7 0.1 broadcast_in_dim.22
  85.8 4.8 %collective-permute-done.15 = f32[328,256]{1,0:T(8,128)S(1)} collective-permute-done((f32[328,256]{1,0:T(8,128)S(1)}, f32[328,256]{1,0:T(8,128)S(1)}, u32[]{:S(2)}, u32[]{:S(2)}) %collective-permute-start.15) | collective-permute-done | bytes 335904 | tf_op jit(solution)/shard_map/ppermute | solution.py:380
  90.7 2.6 %collective-permute-done.16 = f32[328,256]{1,0:T(8,128)S(1)} collective-permute-done((f32[328,256]{1,0:T(8,128)S(1)}, f32[328,256]{1,0:T(8,128)S(1)}, u32[]{:S(2)}, u32[]{:S(2)}) %collective-permute-start.16) | collective-permute-done | bytes 335904 | tf_op jit(solution)/shard_map/ppermute | solution.py:380
  93.2 3.5 %collective-permute-done.17 = f32[328,256]{1,0:T(8,128)S(1)} collective-permute-done((f32[328,256]{1,0:T(8,128)S(1)}, f32[328,256]{1,0:T(8,128)S(1)}, u32[]{:S(2)}, u32[]{:S(2)}) %collective-permute-start.17) | collective-permute-done | bytes 335904 | tf_op jit(solution)/shard_map/ppermute | solution.py:380
  96.8 0.6 dynamic_slice.39
  97.4 0.6 dynamic_slice.38
  98.0 0.0 copy-start.10
  98.1 1.0 %copy-done.10 = f32[1280,256]{1,0:T(8,128)} copy-done((f32[1280,256]{1,0:T(8,128)}, f32[1280,256]{1,0:T(8,128)S(1)}, u32[]{:S(2)}) %copy-start.10) | copy-done | bytes 1310744
  (28 shorter events, 0.4 us)
Async XLA Ops:
  2.0 0.8 copy-start.5
  2.8 4.7 %copy-start = (bf16[1,256,2560]{2,1,0:T(8,128)(2,1)S(1)}, bf16[1,256,2560]{2,1,0:T(8,128)(2,1)}, u32[]{:S(2)}) copy-start(bf16[1,256,2560]{2,1,0:T(8,128)(2,1)} %param.9) | copy-start | bytes 3932164
  2.8 4.7 %copy-start.1 = (bf16[1,256,2560]{2,1,0:T(8,128)(2,1)S(1)}, bf16[1,256,2560]{2,1,0:T(8,128)(2,1)}, u32[]{:S(2)}) copy-start(bf16[1,256,2560]{2,1,0:T(8,128)(2,1)} %param.10) | copy-start | bytes 3932164
  7.3 3.1 %copy-start.7 = (f32[5,256,8]{2,1,0:T(8,128)}, f32[5,256,8]{2,1,0:T(8,128)S(1)}, u32[]{:S(2)}) copy-start(f32[5,256,8]{2,1,0:T(8,128)S(1)} %get-tuple-element.18.cols_ref) | copy-start | bytes 122884
  7.4 3.1 %collective-permute-start = (f32[128,2560]{1,0:T(8,128)S(1)}, f32[128,2560]{1,0:T(8,128)S(1)}, u32[]{:S(2)}, u32[]{:S(2)}) collective-permute-start(f32[128,2560]{1,0:T(8,128)S(1)} %get-tuple-element.20), channel_id=1, source_target_pairs={{0,128},{128,0},{1,129},{129,1},{2,130},{130,2},{3,131},{131,3},{4... | collective-permute-start | bytes 3932168 | tf_op jit(solution)/shard_map/ppermute | solution.py:413
  10.5 1.1 %copy-start.2 = (f32[128,2560]{1,0:T(8,128)}, f32[128,2560]{1,0:T(8,128)S(1)}, u32[]{:S(2)}) copy-start(f32[128,2560]{1,0:T(8,128)S(1)} %collective-permute-done.state_ref) | copy-start | bytes 3932164
  11.5 5.9 %copy-start.11 = (f32[40]{0:T(128)S(1)}, f32[40]{0:T(128)}, u32[]{:S(2)}) copy-start(f32[40]{0:T(128)} %param.14) | copy-start | bytes 484
  15.9 1.1 %copy-start.4 = (f32[1280,256]{1,0:T(8,128)}, f32[1280,256]{1,0:T(8,128)S(1)}, u32[]{:S(2)}) copy-start(f32[1280,256]{1,0:T(8,128)S(1)} %get-tuple-element.26) | copy-start | bytes 3932164
  17.0 3.4 %collective-permute-start.1 = (f32[1280,256]{1,0:T(8,128)}, f32[1280,256]{1,0:T(8,128)}, u32[]{:S(2)}, u32[]{:S(2)}) collective-permute-start(f32[1280,256]{1,0:T(8,128)} %get-tuple-element.27), channel_id=1, source_target_pairs={{0,128},{128,0},{1,129},{129,1},{2,130},{130,2},{3,131},{131,3},{4... | collective-permute-start | bytes 3932168 | tf_op jit(solution)/shard_map/ppermute | solution.py:413
  20.4 6.1 %copy-start.8 = (f32[5,256,8]{2,1,0:T(8,128)S(1)}, f32[5,256,8]{2,1,0:T(8,128)}, u32[]{:S(2)}) copy-start(f32[5,256,8]{2,1,0:T(8,128)} %copy-done.7) | copy-start | bytes 122884
  22.4 15.2 %copy-start.9 = (f32[1280,256]{1,0:T(8,128)}, f32[1280,256]{1,0:T(8,128)S(1)}, u32[]{:S(2)}) copy-start(f32[1280,256]{1,0:T(8,128)S(1)} %add.141) | copy-start | bytes 3932164
  22.4 4.1 %copy-start.3 = (f32[128,2560]{1,0:T(8,128)S(1)}, f32[128,2560]{1,0:T(8,128)}, u32[]{:S(2)}) copy-start(f32[128,2560]{1,0:T(8,128)} %copy-done.2) | copy-start | bytes 3932164
  22.4 4.1 %copy-start.6 = (f32[1,40,256]{2,1,0:T(8,128)S(1)}, f32[1,40,256]{2,1,0:T(8,128)}, u32[]{:S(2)}) copy-start(f32[1,40,256]{2,1,0:T(8,128)} %param.11) | copy-start | bytes 122884
  23.4 17.1 %collective-permute-start.2 = (f32[320,256]{1,0:T(8,128)}, f32[320,256]{1,0:T(8,128)S(1)}, u32[]{:S(2)}, u32[]{:S(2)}) collective-permute-start(f32[320,256]{1,0:T(8,128)} %get-tuple-element.29), channel_id=1, source_target_pairs={{0,1},{1,2},{2,3},{3,0},{4,5},{5,6},{6,7},{7,4},{8,9},{9,10},{10,1... | collective-permute-start | bytes 983048 | tf_op jit(solution)/shard_map/ppermute | solution.py:380
  25.6 14.9 %collective-permute-start.3 = (f32[320,256]{1,0:T(8,128)}, f32[320,256]{1,0:T(8,128)}, u32[]{:S(2)}, u32[]{:S(2)}) collective-permute-start(f32[320,256]{1,0:T(8,128)} %get-tuple-element.31), channel_id=1, source_target_pairs={{0,2},{1,3},{2,0},{3,1},{4,6},{5,7},{6,4},{7,5},{8,10},{9,11},{10,... | collective-permute-start | bytes 983048 | tf_op jit(solution)/shard_map/ppermute | solution.py:380
  26.3 17.8 %collective-permute-start.4 = (f32[320,256]{1,0:T(8,128)}, f32[320,256]{1,0:T(8,128)}, u32[]{:S(2)}, u32[]{:S(2)}) collective-permute-start(f32[320,256]{1,0:T(8,128)} %get-tuple-element.30), channel_id=1, source_target_pairs={{0,3},{1,0},{2,1},{3,2},{4,7},{5,4},{6,5},{7,6},{8,11},{9,8},{10,9... | collective-permute-start | bytes 983048 | tf_op jit(solution)/shard_map/ppermute | solution.py:380
  37.5 1.2 %collective-permute-start.5 = (f32[8,256]{1,0:T(8,128)S(1)}, f32[8,256]{1,0:T(8,128)S(1)}, u32[]{:S(2)}, u32[]{:S(2)}) collective-permute-start(f32[8,256]{1,0:T(8,128)S(1)} %get-tuple-element.28), channel_id=1, source_target_pairs={{0,128},{128,0},{1,129},{129,1},{2,130},{130,2},{3,131},{131,3},{4... | collective-permute-start | bytes 24584 | tf_op jit(solution)/shard_map/ppermute | solution.py:413
  45.5 7.8 %collective-permute-start.6 = (f32[88,256]{1,0:T(8,128)S(1)}, f32[88,256]{1,0:T(8,128)S(1)}, u32[]{:S(2)}, u32[]{:S(2)}) collective-permute-start(f32[88,256]{1,0:T(8,128)S(1)} %get-tuple-element.38), channel_id=1, source_target_pairs={{0,4},{1,5},{2,6},{3,7},{4,8},{5,9},{6,10},{7,11},{8,12},{9,13},{1... | collective-permute-start | bytes 270344 | tf_op jit(solution)/shard_map/ppermute | solution.py:380
  45.6 7.7 %collective-permute-start.7 = (f32[88,256]{1,0:T(8,128)S(1)}, f32[88,256]{1,0:T(8,128)S(1)}, u32[]{:S(2)}, u32[]{:S(2)}) collective-permute-start(f32[88,256]{1,0:T(8,128)S(1)} %get-tuple-element.39), channel_id=1, source_target_pairs={{0,8},{1,9},{2,10},{3,11},{4,12},{5,13},{6,14},{7,15},{8,0},{9,1},... | collective-permute-start | bytes 270344 | tf_op jit(solution)/shard_map/ppermute | solution.py:380
  48.3 5.5 %collective-permute-start.8 = (f32[88,256]{1,0:T(8,128)S(1)}, f32[88,256]{1,0:T(8,128)S(1)}, u32[]{:S(2)}, u32[]{:S(2)}) collective-permute-start(f32[88,256]{1,0:T(8,128)S(1)} %get-tuple-element.40), channel_id=1, source_target_pairs={{0,12},{1,13},{2,14},{3,15},{4,0},{5,1},{6,2},{7,3},{8,4},{9,5},{1... | collective-permute-start | bytes 270344 | tf_op jit(solution)/shard_map/ppermute | solution.py:380
  53.9 4.6 %collective-permute-start.9 = (f32[88,256]{1,0:T(8,128)S(1)}, f32[88,256]{1,0:T(8,128)S(1)}, u32[]{:S(2)}, u32[]{:S(2)}) collective-permute-start(f32[88,256]{1,0:T(8,128)S(1)} %fusion.2), channel_id=1, source_target_pairs={{0,16},{1,17},{2,18},{3,19},{4,20},{5,21},{6,22},{7,23},{8,24},{9,... | collective-permute-start | bytes 270344 | tf_op jit(solution)/shard_map/ppermute | solution.py:433
  58.5 6.5 %collective-permute-start.10 = (f32[88,256]{1,0:T(8,128)S(1)}, f32[88,256]{1,0:T(8,128)S(1)}, u32[]{:S(2)}, u32[]{:S(2)}) collective-permute-start(f32[88,256]{1,0:T(8,128)S(1)} %add.165), channel_id=1, source_target_pairs={{0,32},{1,33},{2,34},{3,35},{4,36},{5,37},{6,38},{7,39},{8,40},{9,... | collective-permute-start | bytes 270344 | tf_op jit(solution)/shard_map/ppermute | solution.py:433
  65.0 9.2 %collective-permute-start.11 = (f32[88,256]{1,0:T(8,128)S(1)}, f32[88,256]{1,0:T(8,128)S(1)}, u32[]{:S(2)}, u32[]{:S(2)}) collective-permute-start(f32[88,256]{1,0:T(8,128)S(1)} %add.166), channel_id=1, source_target_pairs={{0,64},{1,65},{2,66},{3,67},{4,68},{5,69},{6,70},{7,71},{8,72},{9,... | collective-permute-start | bytes 270344 | tf_op jit(solution)/shard_map/ppermute | solution.py:433
  74.3 5.7 %collective-permute-start.12 = (f32[80,256]{1,0:T(8,128)S(1)}, f32[80,256]{1,0:T(8,128)S(1)}, u32[]{:S(2)}, u32[]{:S(2)}) collective-permute-start(f32[80,256]{1,0:T(8,128)S(1)} %get-tuple-element.36), channel_id=1, source_target_pairs={{0,4},{1,5},{2,6},{3,7},{4,8},{5,9},{6,10},{7,11},{8,12},{9,13},{1... | collective-permute-start | bytes 245768 | tf_op jit(solution)/shard_map/ppermute | solution.py:380
  76.1 6.2 %collective-permute-start.13 = (f32[80,256]{1,0:T(8,128)S(1)}, f32[80,256]{1,0:T(8,128)S(1)}, u32[]{:S(2)}, u32[]{:S(2)}) collective-permute-start(f32[80,256]{1,0:T(8,128)S(1)} %get-tuple-element.36), channel_id=1, source_target_pairs={{0,8},{1,9},{2,10},{3,11},{4,12},{5,13},{6,14},{7,15},{8,0},{9,1},... | collective-permute-start | bytes 245768 | tf_op jit(solution)/shard_map/ppermute | solution.py:380
  78.9 4.4 %collective-permute-start.14 = (f32[80,256]{1,0:T(8,128)S(1)}, f32[80,256]{1,0:T(8,128)S(1)}, u32[]{:S(2)}, u32[]{:S(2)}) collective-permute-start(f32[80,256]{1,0:T(8,128)S(1)} %get-tuple-element.36), channel_id=1, source_target_pairs={{0,12},{1,13},{2,14},{3,15},{4,0},{5,1},{6,2},{7,3},{8,4},{9,5},{1... | collective-permute-start | bytes 245768 | tf_op jit(solution)/shard_map/ppermute | solution.py:380
  83.4 7.2 %collective-permute-start.15 = (f32[328,256]{1,0:T(8,128)S(1)}, f32[328,256]{1,0:T(8,128)S(1)}, u32[]{:S(2)}, u32[]{:S(2)}) collective-permute-start(f32[328,256]{1,0:T(8,128)S(1)} %pad_maximum_fusion), channel_id=1, source_target_pairs={{0,1},{1,2},{2,3},{3,0},{4,5},{5,6},{6,7},{7,4},{8,9},{9,10},{10,1... | collective-permute-start | bytes 1007624 | tf_op jit(solution)/shard_map/ppermute | solution.py:380
  84.5 8.8 %collective-permute-start.16 = (f32[328,256]{1,0:T(8,128)S(1)}, f32[328,256]{1,0:T(8,128)S(1)}, u32[]{:S(2)}, u32[]{:S(2)}) collective-permute-start(f32[328,256]{1,0:T(8,128)S(1)} %pad_maximum_fusion), channel_id=1, source_target_pairs={{0,2},{1,3},{2,0},{3,1},{4,6},{5,7},{6,4},{7,5},{8,10},{9,11},{10,... | collective-permute-start | bytes 1007624 | tf_op jit(solution)/shard_map/ppermute | solution.py:380
  85.6 11.2 %collective-permute-start.17 = (f32[328,256]{1,0:T(8,128)S(1)}, f32[328,256]{1,0:T(8,128)S(1)}, u32[]{:S(2)}, u32[]{:S(2)}) collective-permute-start(f32[328,256]{1,0:T(8,128)S(1)} %pad_maximum_fusion), channel_id=1, source_target_pairs={{0,3},{1,0},{2,1},{3,2},{4,7},{5,4},{6,5},{7,6},{8,11},{9,8},{10,9... | collective-permute-start | bytes 1007624 | tf_op jit(solution)/shard_map/ppermute | solution.py:380
  98.0 1.1 %copy-start.10 = (f32[1280,256]{1,0:T(8,128)}, f32[1280,256]{1,0:T(8,128)S(1)}, u32[]{:S(2)}) copy-start(f32[1280,256]{1,0:T(8,128)S(1)} %slice_dynamic-update-slice_fusion) | copy-start | bytes 3932164

commit v2 on v1

v2 whole, which is shorter than its diff:
```python
import jax
import jax.numpy as jnp
from jax import lax
from jax.experimental import pallas as pl
from jax.experimental.pallas import tpu as pltpu
from jax.sharding import PartitionSpec as P

F32 = jnp.float32
BF16 = jnp.bfloat16
HEADS = 40
WIDTH = 64
STATE = 128
TOK = 256
FEAT = HEADS * WIDTH
SCENES = 128
STEP_HEADS = 8
GROUPS = HEADS // STEP_HEADS
STEP_FEAT = STEP_HEADS * WIDTH
HALF = FEAT // 2
MIB = 1024 * 1024
RING = 4
PIECE = HALF // RING
PLANE = RING * RING
ROWS = HALF // PLANE

NN = (((1,), (0,)), ((), ()))
NT = (((1,), (1,)), ((), ()))
TN = (((0,), (0,)), ((), ()))


def dot(a, b, dims):
    return lax.dot_general(a, b, dims, preferred_element_type=F32)


def split2(v):
    high = v.astype(BF16)
    return high, (v - high.astype(F32)).astype(BF16)


def split3(v):
    rows = v.shape[0]
    high = v.astype(BF16).astype(F32)
    rest = v - high
    mid = rest.astype(BF16).astype(F32)
    low = rest - mid
    parts = [high, mid, low]
    extra = -3 * rows % 16
    if extra:
        parts.append(jnp.zeros((extra, v.shape[1]), F32))
    return jnp.concatenate(parts, axis=0)


def dot3(a, b, dims):
    ah, al = split2(a)
    bh, bl = split2(b)
    return dot(ah, bh, dims) + dot(al, bh, dims) + dot(ah, bl, dims)


def head_rows(rows, heads, width):
    row = lax.broadcasted_iota(jnp.int32, (rows, width), 0)
    head = lax.broadcasted_iota(jnp.int32, (rows, width), 1) // WIDTH
    hit = (head == row) | (head == row - heads) | (head == row - 2 * heads)
    return jnp.where(hit & (row < 3 * heads), 1.0, 0.0)


def spread_heads(v, width):
    parts = split3(v).astype(BF16)
    return dot(parts, head_rows(parts.shape[0], v.shape[0], width).astype(BF16), TN)


def turn_column(row):
    same = lax.broadcasted_iota(jnp.int32, (HEADS, HEADS), 0) == lax.broadcasted_iota(jnp.int32, (HEADS, HEADS), 1)
    return jnp.sum(jnp.where(same, row, 0.0), axis=1, keepdims=True)


def sum_parts(v, heads):
    return v[:heads] + v[heads : 2 * heads] + v[2 * heads : 3 * heads]


def state_kernel(
    tile_ref, hidden_hbm, weight_hbm, x_hbm, g_hbm, step_hbm, rate_ref,
    proj_ref, run_ref, cols_ref, scale_ref, rates_ref, high_ref, low_ref, send_ref, wide_ref,
    hidden, weight, values, step_vm, sems,
):
    role = lax.axis_index("seq")
    take_step = pltpu.make_async_copy(step_hbm, step_vm, sems.at[2 * GROUPS + 1])
    take_step.start()
    copies = []
    for c in range(GROUPS):
        part = pl.ds(c * STEP_FEAT, STEP_FEAT)
        copies.append(pltpu.make_async_copy(hidden_hbm.at[:, part], hidden.at[:, part], sems.at[c]))
        copies.append(pltpu.make_async_copy(weight_hbm.at[part], weight.at[part], sems.at[GROUPS + c]))
    for copy in copies:
        copy.start()
    take_x = pltpu.make_async_copy(x_hbm, values, sems.at[2 * GROUPS])
    take_g = pltpu.make_async_copy(g_hbm, values, sems.at[2 * GROUPS])

    @pl.when(role == 0)
    def _():
        take_x.start()

    @pl.when(role != 0)
    def _():
        take_g.start()

    present = jnp.where(tile_ref[0, 0] == 0, 1.0, 0.0).astype(F32)
    take_step.wait()
    step = step_vm[...]
    rate = -jnp.exp(turn_column(rate_ref[...]))
    rates_ref[...] = jnp.broadcast_to(rate, (HEADS, 128))
    logs = step * present * rate
    row = lax.broadcasted_iota(jnp.int32, (TOK, TOK), 0)
    col = lax.broadcasted_iota(jnp.int32, (TOK, TOK), 1)
    upto = jnp.where(row <= col, 1.0, 0.0).astype(BF16)
    run = sum_parts(dot(split3(logs).astype(BF16), upto, NN), HEADS)
    run_ref[...] = run
    less = run - jnp.log(step)
    turned = jnp.concatenate([less, jnp.zeros((STATE - HEADS, TOK), F32)], axis=0).T
    for k in range(GROUPS):
        cols_ref[k] = turned[:, k * STEP_HEADS : (k + 1) * STEP_HEADS]
    tail = step * jnp.exp(run[:, TOK - 1 :] - run)
    scale = jnp.where(role == 0, tail, jnp.exp(run)) * present
    scale_ref[...] = scale

    proj = jnp.zeros((TOK, 2 * STATE), F32)
    for c in range(GROUPS):
        copies[2 * c].wait()
        copies[2 * c + 1].wait()
        part = slice(c * STEP_FEAT, (c + 1) * STEP_FEAT)
        proj = proj + dot(hidden[:, part], weight[part, :], NN)
    proj_ref[...] = proj
    mine = jnp.where(role == 0, proj[:, :STATE], proj[:, STATE:])
    mine_high, mine_low = split2(mine)
    take_x.wait()
    parts = split3(scale).astype(BF16)
    for c in range(GROUPS):
        part = slice(c * STEP_FEAT, (c + 1) * STEP_FEAT)
        r = lax.broadcasted_iota(jnp.int32, (parts.shape[0], STEP_FEAT), 0)
        h = lax.broadcasted_iota(jnp.int32, (parts.shape[0], STEP_FEAT), 1) // WIDTH + c * STEP_HEADS
        hit = (h == r) | (h == r - HEADS) | (h == r - 2 * HEADS)
        pick = jnp.where(hit, 1.0, 0.0).astype(BF16)
        scaled = dot(parts, pick, TN) * values[:, part].astype(F32)
        high, low = split2(scaled)
        high_ref[:, part] = high
        low_ref[:, part] = low
        send_ref[:, part] = dot(mine_high, high, TN) + dot(mine_low, high, TN) + dot(mine_high, low, TN)
    for c in range(GROUPS):
        lanes = pl.ds(pl.multiple_of((1 - role) * HALF + c * 256, 128), 256)
        wide_ref[:, c * 256 : (c + 1) * 256] = hidden[:, lanes].astype(F32)


def state_call(tile, hidden, weight, x, g, step, log_rate):
    sm = pl.BlockSpec(memory_space=pltpu.SMEM)
    vm = pl.BlockSpec(memory_space=pltpu.VMEM)
    hbm = pl.BlockSpec(memory_space=pltpu.HBM)
    return pl.pallas_call(
        state_kernel,
        name="state_to_send",
        out_shape=(
            jax.ShapeDtypeStruct((TOK, 2 * STATE), F32),
            jax.ShapeDtypeStruct((HEADS, TOK), F32),
            jax.ShapeDtypeStruct((GROUPS, TOK, STEP_HEADS), F32),
            jax.ShapeDtypeStruct((HEADS, TOK), F32),
            jax.ShapeDtypeStruct((HEADS, 128), F32),
            jax.ShapeDtypeStruct((TOK, FEAT), BF16),
            jax.ShapeDtypeStruct((TOK, FEAT), BF16),
            jax.ShapeDtypeStruct((STATE, FEAT), F32),
            jax.ShapeDtypeStruct((TOK, HALF), F32),
        ),
        in_specs=[sm] + [hbm] * 5 + [vm],
        out_specs=(vm,) * 9,
        scratch_shapes=[
            pltpu.VMEM((TOK, FEAT), BF16),
            pltpu.VMEM((FEAT, 2 * STATE), BF16),
            pltpu.VMEM((TOK, FEAT), BF16),
            pltpu.VMEM((HEADS, TOK), F32),
            pltpu.SemaphoreType.DMA((2 * GROUPS + 2,)),
        ],
        compiler_params=pltpu.CompilerParams(vmem_limit_bytes=48 * MIB),
        cost_estimate=pl.CostEstimate(flops=1_000_000_000, bytes_accessed=8_000_000, transcendentals=20_000),
    )(tile, hidden, weight, x, g, step, log_rate)


def causal_bias():
    row = lax.broadcasted_iota(jnp.int32, (STATE, STATE), 0)
    col = lax.broadcasted_iota(jnp.int32, (STATE, STATE), 1)
    return jnp.where(col >= row, 0.0, -1e30).astype(F32)


def own_half(v, which):
    lane = lax.broadcasted_iota(jnp.int32, v.shape, 1)
    keep = (lane < WIDTH) if which == 0 else (lane >= WIDTH)
    return jnp.where(keep, v, jnp.zeros_like(v))


def decays(run_row, less_col, bias):
    d = run_row - less_col
    first = jnp.exp(jnp.concatenate([d[:STATE, :STATE] + bias, d[:STATE, STATE:]], axis=1))
    second = jnp.exp(d[STATE:, STATE:] + bias)
    return first, second


def pair_kernel(x_ref, g_ref, run_ref, cols_ref, out_ref):
    bias = causal_bias()
    first = jnp.zeros((STATE, TOK), F32)
    second = jnp.zeros((STATE, STATE), F32)
    for q in range(STEP_HEADS // 2):
        lanes = slice(q * 128, q * 128 + 128)
        x, g = x_ref[:, lanes], g_ref[:, lanes]
        w = dot(jnp.concatenate([own_half(x, 0), own_half(x, 1)], axis=0), g, NT)
        for half in range(2):
            r = 2 * q + half
            d1, d2 = decays(run_ref[r : r + 1, :], cols_ref[0][:, r : r + 1], bias)
            first = first + d1 * w[half * TOK : half * TOK + STATE]
            second = second + d2 * w[half * TOK + STATE : half * TOK + TOK, STATE:]

    @pl.when(pl.program_id(0) == 0)
    def _():
        out_ref[...] = jnp.zeros_like(out_ref)

    out_ref[:STATE, :] += first
    out_ref[STATE:, STATE:] += second


def pair_call(x, g, run, cols):
    return pl.pallas_call(
        pair_kernel,
        name="score_gradient",
        grid=(GROUPS,),
        out_shape=jax.ShapeDtypeStruct((TOK, TOK), F32),
        in_specs=[
            pl.BlockSpec((TOK, STEP_FEAT), lambda k: (0, k)),
            pl.BlockSpec((TOK, STEP_FEAT), lambda k: (0, k)),
            pl.BlockSpec((STEP_HEADS, TOK), lambda k: (k, 0)),
            pl.BlockSpec((1, TOK, STEP_HEADS), lambda k: (k, 0, 0)),
        ],
        out_specs=pl.BlockSpec((TOK, TOK), lambda k: (0, 0)),
        compiler_params=pltpu.CompilerParams(vmem_limit_bytes=16 * MIB),
        cost_estimate=pl.CostEstimate(flops=1_500_000_000, bytes_accessed=3_000_000, transcendentals=2_600_000),
    )(x, g, run, cols)


def proj_kernel(tile_ref, pair_ref, proj_ref, high_ref, low_ref, state_ref, grad_ref):
    role = lax.axis_index("seq")
    present = jnp.where(tile_ref[0, 0] == 0, 1.0, 0.0).astype(F32)
    pair = pair_ref[...] * present
    proj = proj_ref[...]
    keys = dot3(pair, proj[:, STATE:], NN)
    query = dot3(pair, proj[:, :STATE], TN)
    both = jnp.concatenate(split2(state_ref[...]), axis=0)
    high = dot(high_ref[...], both, NT)
    across = high[:, :STATE] + high[:, STATE:] + dot(low_ref[...], both[:STATE], NT)
    keys = keys + jnp.where(role == 0, across, 0.0)
    query = query + jnp.where(role == 0, 0.0, across)
    grad_ref[...] = jnp.concatenate([keys, query], axis=1) * (1.0 / SCENES)


def proj_call(tile, pair, proj, high, low, state):
    vm = pl.BlockSpec(memory_space=pltpu.VMEM)
    return pl.pallas_call(
        proj_kernel,
        name="proj_gradient",
        out_shape=jax.ShapeDtypeStruct((TOK, 2 * STATE), F32),
        in_specs=[pl.BlockSpec(memory_space=pltpu.SMEM)] + [vm] * 5,
        out_specs=vm,
        compiler_params=pltpu.CompilerParams(vmem_limit_bytes=16 * MIB),
        cost_estimate=pl.CostEstimate(flops=700_000_000, bytes_accessed=4_000_000, transcendentals=0),
    )(tile, pair, proj, high, low, state)


def ring_place():
    role = lax.axis_index("seq")
    chip = lax.axis_index("dp")
    x, y = chip % 4, chip // 4 % 4
    return jnp.where(role == 0, x, y), jnp.where(role == 0, y, x)


def weight_kernel(grad_ref, other_ref, hidden_ref, wide_ref, *refs):
    outs, sums = refs[:RING], refs[RING]
    role = lax.axis_index("seq")
    own = jnp.concatenate(split2(grad_ref[...]), axis=1)
    other = jnp.concatenate(split2(other_ref[...]), axis=1)
    chunk = 256
    for c in range(HALF // chunk):
        lanes = pl.ds(pl.multiple_of(role * HALF + c * chunk, 128), chunk)
        got = dot(hidden_ref[:, lanes], own, TN)
        got = got + dot(wide_ref[:, c * chunk : (c + 1) * chunk].astype(BF16), other, TN)
        sums[c * chunk : (c + 1) * chunk, :] = got[:, : 2 * STATE] + got[:, 2 * STATE :]
    me, _ = ring_place()
    for k in range(RING):
        place = lax.rem(me + k, RING) * PIECE
        outs[k][...] = sums[pl.ds(pl.multiple_of(place, 8), PIECE), :]


def weight_call(grad, other, hidden, wide):
    vm = pl.BlockSpec(memory_space=pltpu.VMEM)
    return pl.pallas_call(
        weight_kernel,
        name="weight_gradient",
        out_shape=[jax.ShapeDtypeStruct((PIECE, 2 * STATE), F32)] * RING,
        in_specs=[vm] * 4,
        out_specs=[vm] * RING,
        scratch_shapes=[pltpu.VMEM((HALF, 2 * STATE), F32)],
        compiler_params=pltpu.CompilerParams(vmem_limit_bytes=16 * MIB),
        cost_estimate=pl.CostEstimate(flops=1_400_000_000, bytes_accessed=4_000_000, transcendentals=0),
    )(grad, other, hidden, wide)


def input_kernel(
    tile_ref, x_ref, g_ref, run_ref, cols_ref, scale_ref, step_ref, rates_ref, gain_ref, state_ref, proj_ref,
    dx_ref, dstep_ref, small_ref,
    scores, rows, mine_terms, sums, gains, slopes, direct, owns,
):
    role = lax.axis_index("seq")
    first_role = jnp.where(role == 0, 1.0, 0.0).astype(F32)
    present = jnp.where(tile_ref[0, 0] == 0, 1.0, 0.0).astype(F32)
    k = pl.program_id(0)

    @pl.when(k == 0)
    def _():
        small_ref[...] = jnp.zeros_like(small_ref)
        scores[...] = dot3(proj_ref[:, :STATE], proj_ref[:, STATE:], NT) * present
        gains[...] = jnp.broadcast_to(turn_column(gain_ref[...]), (HEADS, 128))
        mine_high, mine_low = split2(jnp.where(role == 0, proj_ref[:, :STATE], proj_ref[:, STATE:]))
        mine_terms[...] = jnp.concatenate([mine_high, mine_low, mine_high], axis=1)

    bias = causal_bias()
    state_high, state_low = split2(state_ref[...])
    carried = dot(mine_terms[...], jnp.concatenate([state_high, state_high, state_low], axis=0), NN)
    carried = carried * spread_heads(scale_ref[...], STEP_FEAT)
    select = head_rows(STEP_HEADS, STEP_HEADS, STEP_FEAT)
    at = pl.ds(pl.multiple_of(k * STEP_HEADS, STEP_HEADS), STEP_HEADS)
    gain_row = jnp.sum(select * gains[at, :1], axis=0, keepdims=True) * present
    x_all = x_ref[...].astype(F32)
    g_all = g_ref[...].astype(F32)
    own = jnp.where(role == 0, x_all, g_all)
    pick = jnp.concatenate([select, jnp.zeros_like(select)], axis=0).astype(BF16)
    own_high, own_low = split2(own * carried)
    by_own = (dot(pick, own_high, NT) + dot(pick, own_low, NT))[:STEP_HEADS]
    within = []
    for q in range(STEP_HEADS // 2):
        lanes = slice(q * 128, q * 128 + 128)
        x = x_ref[:, lanes]
        upper = jnp.zeros((STATE, 128), F32)
        lower = jnp.zeros((STATE, 128), F32)
        for half in range(2):
            r = 2 * q + half
            g = own_half(g_ref[:, lanes], half)
            d1, d2 = decays(run_ref[r : r + 1, :], cols_ref[0][:, r : r + 1], bias)
            m1 = d1 * scores[:STATE, :]
            m2 = d2 * scores[STATE:, STATE:]
            f1 = m1 * dot(x[:STATE], g, NT)
            f2 = m2 * dot(x[STATE:], g[STATE:], NT)
            sums[:STATE, r : r + 1] = jnp.sum(f1, axis=1, keepdims=True)
            sums[STATE:, r : r + 1] = jnp.sum(f2, axis=1, keepdims=True)
            f1 = jnp.sum(f1, axis=0, keepdims=True)
            f2 = jnp.sum(f2, axis=0, keepdims=True)
            rows[r : r + 1, :STATE] = f1[:, :STATE]
            rows[r : r + 1, STATE:] = f1[:, STATE:] + f2
            h1, l1 = split2(m1)
            h2, l2 = split2(m2)
            upper = upper + dot(h1, g, NN) + dot(l1, g, NN)
            lower = lower + dot(h2, g[STATE:], NN) + dot(l2, g[STATE:], NN)
        within.append(jnp.concatenate([upper, lower], axis=0))
    total = jnp.concatenate(within, axis=1) + first_role * carried
    dx_ref[...] = (total + gain_row * g_all).astype(BF16)

    r8 = lax.broadcasted_iota(jnp.int32, (8, 128), 0)
    lane = lax.broadcasted_iota(jnp.int32, (8, 128), 1)
    gx = jnp.sum(g_all * x_all, axis=0, keepdims=True) * present
    d_gain = jnp.sum(select * gx, axis=1, keepdims=True) * (1.0 / SCENES)
    small_ref[:, 128:] += jnp.where(lane == r8 + k * STEP_HEADS, d_gain, 0.0)
    columns = sums[...].T[:STEP_HEADS]
    direct[at, :] = columns + first_role * by_own
    slopes[at, :] = rows[...] - columns + (1.0 - 2.0 * first_role) * by_own
    owns[at, :] = by_own

    @pl.when(k == GROUPS - 1)
    def _():
        row = lax.broadcasted_iota(jnp.int32, (TOK, TOK), 0)
        col = lax.broadcasted_iota(jnp.int32, (TOK, TOK), 1)
        after = jnp.where(row >= col, 1.0, 0.0).astype(BF16)
        logs = sum_parts(dot(split3(slopes[...]).astype(BF16), after, NN), HEADS)
        logs = logs + first_role * jnp.sum(owns[...], axis=1, keepdims=True)
        step = step_ref[...]
        rate = rates_ref[:, :1]
        dstep_ref[...] = direct[...] / step + rate * logs
        d_rate = rate * present * jnp.sum(step * logs, axis=1, keepdims=True) * (1.0 / SCENES)
        for t in range(GROUPS):
            part = d_rate[t * STEP_HEADS : (t + 1) * STEP_HEADS]
            small_ref[:, :128] += jnp.where(lane == r8 + t * STEP_HEADS, part, 0.0)


def input_call(tile, x, g, run, cols, scale, step, rates, gain, state, proj):
    feat = pl.BlockSpec((TOK, STEP_FEAT), lambda k: (0, k))
    head = pl.BlockSpec((STEP_HEADS, TOK), lambda k: (k, 0))
    return pl.pallas_call(
        input_kernel,
        name="input_gradient",
        grid=(GROUPS,),
        out_shape=(
            jax.ShapeDtypeStruct((TOK, FEAT), BF16),
            jax.ShapeDtypeStruct((HEADS, TOK), F32),
            jax.ShapeDtypeStruct((8, 256), F32),
        ),
        in_specs=[
            pl.BlockSpec(memory_space=pltpu.SMEM),
            feat,
            feat,
            head,
            pl.BlockSpec((1, TOK, STEP_HEADS), lambda k: (k, 0, 0)),
            head,
            pl.BlockSpec((HEADS, TOK), lambda k: (0, 0)),
            pl.BlockSpec((HEADS, 128), lambda k: (0, 0)),
            pl.BlockSpec((1, HEADS), lambda k: (0, 0)),
            pl.BlockSpec((STATE, STEP_FEAT), lambda k: (0, k)),
            pl.BlockSpec((TOK, 2 * STATE), lambda k: (0, 0)),
        ],
        out_specs=(feat, pl.BlockSpec((HEADS, TOK), lambda k: (0, 0)), pl.BlockSpec((8, 256), lambda k: (0, 0))),
        scratch_shapes=[
            pltpu.VMEM((TOK, TOK), F32),
            pltpu.VMEM((STEP_HEADS, TOK), F32),
            pltpu.VMEM((TOK, 3 * STATE), BF16),
            pltpu.VMEM((TOK, 128), F32),
            pltpu.VMEM((HEADS, 128), F32),
            pltpu.VMEM((HEADS, TOK), F32),
            pltpu.VMEM((HEADS, TOK), F32),
            pltpu.VMEM((HEADS, TOK), F32),
        ],
        compiler_params=pltpu.CompilerParams(vmem_limit_bytes=16 * MIB),
        cost_estimate=pl.CostEstimate(flops=6_000_000_000, bytes_accessed=8_000_000, transcendentals=2_600_000),
    )(tile, x, g, run, cols, scale, step, rates, gain, state, proj)


def last_kernel(pieces_ref, out_ref, rate_ref, gain_ref, small, sems):
    role = lax.axis_index("seq")
    few = pltpu.make_async_copy(pieces_ref.at[:, pl.ds(ROWS, 8)], small, sems.at[PLANE])
    few.start()
    copies = []
    for j in range(PLANE):
        place = jnp.where(role == 0, j % RING * RING + j // RING, j)
        copies.append(pltpu.make_async_copy(pieces_ref.at[j, pl.ds(0, ROWS)], out_ref.at[place], sems.at[j]))
    for copy in copies:
        copy.start()
    few.wait()
    total = jnp.sum(jnp.sum(small[...], axis=0), axis=0, keepdims=True)
    share = HEADS // 2
    rate_ref[...] = jnp.where(role == 0, total[:, :share], total[:, share:HEADS])
    gain_ref[...] = jnp.where(role == 0, total[:, 128 : 128 + share], total[:, 128 + share : 128 + HEADS])
    for copy in copies:
        copy.wait()


def last_call(pieces):
    hbm = pl.BlockSpec(memory_space=pl.ANY)
    vm = pl.BlockSpec(memory_space=pltpu.VMEM)
    return pl.pallas_call(
        last_kernel,
        name="weight_rows",
        out_shape=(
            jax.ShapeDtypeStruct((PLANE, ROWS, 2 * STATE), F32),
            jax.ShapeDtypeStruct((1, HEADS // 2), F32),
            jax.ShapeDtypeStruct((1, HEADS // 2), F32),
        ),
        in_specs=[hbm],
        out_specs=(hbm, vm, vm),
        scratch_shapes=[pltpu.VMEM((PLANE, 8, 2 * STATE), F32), pltpu.SemaphoreType.DMA((PLANE + 1,))],
        compiler_params=pltpu.CompilerParams(vmem_limit_bytes=16 * MIB),
        cost_estimate=pl.CostEstimate(flops=10_000, bytes_accessed=2_600_000, transcendentals=0),
    )(pieces)


STRIDE = {"z": 16, "y": 4, "x": 1}


def moved(chip, axis, size, new):
    c = chip // STRIDE[axis] % size
    return chip + (new(c) - c) * STRIDE[axis]


def ring_shift(v, stage, k):
    pairs = []
    for core, axes in enumerate(("xy", "yx")):
        for chip in range(SCENES):
            to = moved(chip, axes[stage], RING, lambda c: (c + k) % RING)
            pairs.append((core * SCENES + chip, core * SCENES + to))
    return lax.ppermute(v, ("seq", "dp"), pairs)


def across_z(v, bit):
    return lax.ppermute(v, "dp", [(i, moved(i, "z", 8, lambda c: c ^ bit)) for i in range(SCENES)])


def swap(v):
    return lax.ppermute(v, "seq", [(0, 1), (1, 0)])


def shards(hidden, scan_input, grad_out, step_size, proj_weight, log_rate, skip_gain, tile_list):
    hid, x, g, step = hidden[0], scan_input[0], grad_out[0], step_size[0]
    proj, run, cols, scale, rates, high, low, send, wide = state_call(
        tile_list, hid, proj_weight, x, g, step, log_rate[None]
    )
    state = swap(send)
    wide = swap(wide)
    pair = pair_call(x, g, run, cols)
    grad = proj_call(tile_list, pair, proj, high, low, state)
    pieces = weight_call(grad, swap(grad), hid, wide)
    _, second = ring_place()
    sent = [ring_shift(pieces[k], 0, k) for k in range(1, RING)]
    dx, dstep, small = input_call(tile_list, x, g, run, cols, scale, step, rates, skip_gain[None], state, proj)
    sent, small = lax.optimization_barrier((sent, small))
    small = small + swap(small)
    part = pieces[0] + sent[0] + sent[1] + sent[2]
    cut = [lax.dynamic_slice_in_dim(part, (second + k) % RING * ROWS, ROWS, 0) for k in range(RING)]
    part = cut[0] + sum(ring_shift(cut[k], 1, k) for k in range(1, RING))
    part = jnp.concatenate([part, small], axis=0)
    for bit in (1, 2, 6):
        part = part + across_z(part, bit)
    plane = [[z * PLANE + i for i in range(PLANE)] for z in range(SCENES // PLANE)]
    pieces = lax.all_to_all(
        jnp.broadcast_to(part, (PLANE,) + part.shape), "dp", 0, 0, axis_index_groups=plane, tiled=True
    )
    grad_weight, d_rate, d_gain = last_call(pieces)
    grad_weight = grad_weight.reshape(HALF, 2 * STATE)
    return dx[None], dstep[None], grad_weight, d_rate[0], d_gain[0]


def solution(mesh):
    in_specs = (
        P("dp", "seq", None),
        P("dp", "seq", None),
        P("dp", "seq", None),
        P("dp", None, "seq"),
        P(),
        P(),
        P(),
        P("dp", "seq"),
    )
    out_specs = (P("dp", "seq", None), P("dp", None, "seq"), P("seq", None), P("seq"), P("seq"))
    return jax.shard_map(shards, mesh=mesh, in_specs=in_specs, out_specs=out_specs, check_vma=False)
```

time: 99.3 us -> 88.5 us (0.89)
  the two profiles are of different devices: /device:TPU:6 before, /device:TPU:32 now
where the time goes in v2:
time: 88.5 us; the launch traced here: 88.3 us
  blocking collectives  23.7 us (27%)
  Pallas kernels  23.4 us (26%)
  starting transfers between devices  21 us (24%)
  waiting for transfers between devices  16.9 us (19%)
  between operations  1.6 us (2%)
  local copies, waits for them, and re-layouts  1.59 us (2%)
    all_to_all x1, blocking collectives, shards(): lax.all_to_all(jnp.broadcast_to(part, (PLANE,) + part.shape), 'dp', 0, 0,...  23.7 us
    ppermute x6, starting transfers between devices, ring_shift(): return lax.ppermute(v, ('seq', 'dp'), pairs)  11 us
    ppermute x3, waiting for transfers between devices, across_z(): lax.ppermute(v, 'dp', [(i, moved(i, 'z', 8, lambda c: c ^ bit)) for i in...  10.8 us
    pallas_call x1, Pallas kernels, input_call(): pl.pallas_call(input_kernel, name='input_gradient', grid=(GROUPS,), out_s...  9.96 us
    ppermute x3, starting transfers between devices, across_z(): lax.ppermute(v, 'dp', [(i, moved(i, 'z', 8, lambda c: c ^ bit)) for i in...  9.13 us
    pallas_call x1, Pallas kernels, state_call(): pl.pallas_call(state_kernel, name='state_to_send', out_shape=(jax.ShapeDt...  5.38 us
    ppermute x6, waiting for transfers between devices, ring_shift(): return lax.ppermute(v, ('seq', 'dp'), pairs)  3.16 us
    ppermute x4, waiting for transfers between devices, swap(): return lax.ppermute(v, 'seq', [(0, 1), (1, 0)])  2.97 us
  transfers between devices with their start and end apart: 13, of which 7 were waited for; matrix products, arithmetic and copies ran while one was open for 0% of the time, Pallas kernels for 16%

profile of v2, /device:TPU:32, one launch (start us, length us, event | category | flops | bytes accessed | tf_op | source)
XLA Modules:
  0.0 88.3 jit_solution(5082484421769482268)
XLA Ops:
  1.3 0.0 copy-start.5
  1.3 0.8 copy-done.5
  2.1 0.0 copy-start.7
  2.1 0.7 copy-done.7
  2.7 0.0 copy-start.1
  2.7 0.0 copy-start.3
  2.7 5.4 %state_to_send.1 = (f32[256,256]{1,0:T(8,128)S(1)}, f32[40,256]{1,0:T(8,128)S(1)}, f32[5,256,8]{2,1,0:T(8,128)S(1)}, f32[40,256]{1,0:T(8,128)S(1)}, f32[40,128]{...) custom-call(s32[1,1]{1,0:T(1,128)S(6)} %copy.13.tile_ref, ...), custom_call_target="tpu_custom_call" | custom-call | flops 1000000000 | bytes 8000000 | tf_op jit(solution)/shard_map/state_to_send/pallas_call | solution.py:156
  8.1 0.0 copy-start.8
  8.1 0.1 collective-permute-start
  8.2 0.5 collective-permute-start.2
  8.7 0.0 copy-done.1
  8.7 0.0 copy-done.3
  8.7 2.9 %score_gradient.1.pair_ref = f32[256,256]{1,0:T(8,128)S(1)} custom-call(bf16[256,2560]{1,0:T(8,128)(2,1)S(1)} %bitcast.14, bf16[256,2560]{1,0:T(8,128)(2,1)S(1)} %bitcast.17, f32[40,256]{1,0:T(8,128)S(1)} %get-tuple-element.28.run_ref, f32[5,256,8]{2,1,0:T(8,128)S(1)} %get-tuple-element.29.cols_ref), custom_call_target="tpu_custom_call" | custom-call | flops 1500000000 | bytes 3000000 | tf_op jit(solution)/shard_map/score_gradient/pallas_call | solution.py:226
  11.7 0.0 copy-done.8
  11.7 0.4 collective-permute-done.state_ref
  12.1 0.0 copy-start
  12.1 1.0 %proj_gradient.1.grad_ref = f32[256,256]{1,0:T(8,128)S(1)} custom-call(s32[1,1]{1,0:T(1,128)S(6)} %copy.13.tile_ref, f32[256,256]{1,0:T(8,128)S(1)} %score_gradient.1.pair_ref, f32[256,256]{1,0:T(8,128)S(1)} %get-tuple-element.33.proj_ref, bf16[256,2560]{1,0:T(8,128)(2,1)S(1)} %get-tuple-element.36.high_ref, ...), custom_call_target="tpu_custom_call" | custom-call | flops 700000000 | bytes 4000000 | tf_op jit(solution)/shard_map/proj_gradient/pallas_call | solution.py:260
  13.2 0.2 collective-permute-start.1
  13.4 0.0 copy-start.2
  13.4 0.0 copy-start.4
  13.4 0.0 copy-start.6
  13.4 0.0 copy-start.9
  13.4 0.0 copy-start.10
  13.4 0.0 collective-permute-done.2.wide_ref
  13.5 1.3 %collective-permute-done.1.other_ref = f32[256,256]{1,0:T(8,128)S(1)} collective-permute-done((f32[256,256]{1,0:T(8,128)S(1)}, f32[256,256]{1,0:T(8,128)S(1)}, u32[]{:S(2)}, u32[]{:S(2)}) %collective-permute-start.1) | collective-permute-done | bytes 262176 | tf_op jit(solution)/shard_map/ppermute | solution.py:495
  14.8 0.0 copy-done
  14.8 2.4 %weight_gradient.1 = (f32[320,256]{1,0:T(8,128)S(1)}, f32[320,256]{1,0:T(8,128)S(1)}, f32[320,256]{1,0:T(8,128)S(1)}, f32[320,256]{1,0:T(8,128)S(1)}) custom-call(f32[256,256]{1,0:T(8,128)S(1)} %proj_gradient.1.grad_ref, f32[256,256]{1,0:T(8,128)S(1)} %collective-permute-done.1.other_ref, bf16[256,2560]{1,0:T(8,128)(2,1)S(1)} %bitcast.12, ...), custom_call_target="tpu_custom_call" | custom-call | flops 1400000000 | bytes 4000000 | tf_op jit(solution)/shard_map/weight_gradient/pallas_call | solution.py:297
  17.1 1.6 %collective-permute-start.3 = (f32[320,256]{1,0:T(8,128)S(1)}, f32[320,256]{1,0:T(8,128)S(1)}, u32[]{:S(2)}, u32[]{:S(2)}) collective-permute-start(f32[320,256]{1,0:T(8,128)S(1)} %get-tuple-element.40), channel_id=1, source_target_pairs={{0,1},{1,2},{2,3},{3,0},{4,5},{5,6},{6,7},{7,4},{8,9},{9,10},{10,1... | collective-permute-start | bytes 983048 | tf_op jit(solution)/shard_map/ppermute | solution.py:487
  18.7 2.7 %collective-permute-start.4 = (f32[320,256]{1,0:T(8,128)S(1)}, f32[320,256]{1,0:T(8,128)S(1)}, u32[]{:S(2)}, u32[]{:S(2)}) collective-permute-start(f32[320,256]{1,0:T(8,128)S(1)} %get-tuple-element.41), channel_id=1, source_target_pairs={{0,2},{1,3},{2,0},{3,1},{4,6},{5,7},{6,4},{7,5},{8,10},{9,11},{10,... | collective-permute-start | bytes 983048 | tf_op jit(solution)/shard_map/ppermute | solution.py:487
  21.4 1.4 %collective-permute-start.5 = (f32[320,256]{1,0:T(8,128)S(1)}, f32[320,256]{1,0:T(8,128)S(1)}, u32[]{:S(2)}, u32[]{:S(2)}) collective-permute-start(f32[320,256]{1,0:T(8,128)S(1)} %get-tuple-element.42), channel_id=1, source_target_pairs={{0,3},{1,0},{2,1},{3,2},{4,7},{5,4},{6,5},{7,6},{8,11},{9,8},{10,9... | collective-permute-start | bytes 983048 | tf_op jit(solution)/shard_map/ppermute | solution.py:487
  22.9 0.0 copy-done.2
  22.9 0.0 copy-done.4
  22.9 0.0 copy-done.6
  22.9 0.0 copy-done.9
  22.9 0.0 copy-done.10
  22.9 10.0 %input_gradient.1 = (bf16[256,2560]{1,0:T(8,128)(2,1)}, f32[40,256]{1,0:T(8,128)}, f32[8,256]{1,0:T(8,128)S(1)}) custom-call(s32[1,1]{1,0:T(1,128)S(6)} %copy.13.tile_ref, bf16[256,2560]{1,0:T(8,128)(2,1)S(1)} %bitcast.15, bf16[256,2560]{1,0:T(8,128)(2,1)S(1)} %bitcast.18, f32[40,256]{1,0:T(8,128)S(1)} %get-tuple-element.28.run_ref, ...), custom_call_target="tpu_custom_call" | custom-call | flops 6000000000 | bytes 8000000 | tf_op jit(solution)/shard_map/input_gradient/pallas_call | solution.py:397
  32.9 0.0 collective-permute-done.3
  32.9 0.0 collective-permute-done.4
  32.9 0.0 collective-permute-done.5
  32.9 0.1 add_add_fusion
  33.0 3.1 %collective-permute-start.8 = (f32[80,256]{1,0:T(8,128)S(1)}, f32[80,256]{1,0:T(8,128)S(1)}, u32[]{:S(2)}, u32[]{:S(2)}) collective-permute-start(f32[80,256]{1,0:T(8,128)S(1)} %get-tuple-element.52), channel_id=1, source_target_pairs={{0,12},{1,13},{2,14},{3,15},{4,0},{5,1},{6,2},{7,3},{8,4},{9,5},{1... | collective-permute-start | bytes 245768 | tf_op jit(solution)/shard_map/ppermute | solution.py:487
  36.1 0.0 collective-permute-start.6
  36.1 2.2 %collective-permute-start.7 = (f32[80,256]{1,0:T(8,128)S(1)}, f32[80,256]{1,0:T(8,128)S(1)}, u32[]{:S(2)}, u32[]{:S(2)}) collective-permute-start(f32[80,256]{1,0:T(8,128)S(1)} %get-tuple-element.51), channel_id=1, source_target_pairs={{0,8},{1,9},{2,10},{3,11},{4,12},{5,13},{6,14},{7,15},{8,0},{9,1},... | collective-permute-start | bytes 245768 | tf_op jit(solution)/shard_map/ppermute | solution.py:487
  38.3 0.0 collective-permute-start.9
  38.3 1.2 %collective-permute-done.9 = f32[8,256]{1,0:T(8,128)S(1)} collective-permute-done((f32[8,256]{1,0:T(8,128)S(1)}, f32[8,256]{1,0:T(8,128)S(1)}, u32[]{:S(2)}, u32[]{:S(2)}) %collective-permute-start.9) | collective-permute-done | bytes 8224 | tf_op jit(solution)/shard_map/ppermute | solution.py:495
  39.5 0.0 collective-permute-done.8
  39.5 3.1 %collective-permute-done.6 = f32[80,256]{1,0:T(8,128)S(1)} collective-permute-done((f32[80,256]{1,0:T(8,128)S(1)}, f32[80,256]{1,0:T(8,128)S(1)}, u32[]{:S(2)}, u32[]{:S(2)}) %collective-permute-start.6) | collective-permute-done | bytes 81952 | tf_op jit(solution)/shard_map/ppermute | solution.py:487
  42.7 0.0 collective-permute-done.7
  42.7 0.2 collective-permute-start.10
  42.9 4.4 %collective-permute-done.10 = f32[88,256]{1,0:T(8,128)S(1)} collective-permute-done((f32[88,256]{1,0:T(8,128)S(1)}, f32[88,256]{1,0:T(8,128)S(1)}, u32[]{:S(2)}, u32[]{:S(2)}) %collective-permute-start.10) | collective-permute-done | bytes 90144 | tf_op jit(solution)/shard_map/ppermute | solution.py:491
  47.3 3.4 %collective-permute-start.11 = (f32[88,256]{1,0:T(8,128)S(1)}, f32[88,256]{1,0:T(8,128)S(1)}, u32[]{:S(2)}, u32[]{:S(2)}) collective-permute-start(f32[88,256]{1,0:T(8,128)S(1)} %fusion), channel_id=1, source_target_pairs={{0,32},{1,33},{2,34},{3,35},{4,36},{5,37},{6,38},{7,39},{8,40},{9,... | collective-permute-start | bytes 270344 | tf_op jit(solution)/shard_map/ppermute | solution.py:491
  50.7 3.0 %collective-permute-done.11 = f32[88,256]{1,0:T(8,128)S(1)} collective-permute-done((f32[88,256]{1,0:T(8,128)S(1)}, f32[88,256]{1,0:T(8,128)S(1)}, u32[]{:S(2)}, u32[]{:S(2)}) %collective-permute-start.11) | collective-permute-done | bytes 90144 | tf_op jit(solution)/shard_map/ppermute | solution.py:491
  53.7 5.6 %collective-permute-start.12 = (f32[88,256]{1,0:T(8,128)S(1)}, f32[88,256]{1,0:T(8,128)S(1)}, u32[]{:S(2)}, u32[]{:S(2)}) collective-permute-start(f32[88,256]{1,0:T(8,128)S(1)} %add.92), channel_id=1, source_target_pairs={{0,96},{1,97},{2,98},{3,99},{4,100},{5,101},{6,102},{7,103},{8,104... | collective-permute-start | bytes 270344 | tf_op jit(solution)/shard_map/ppermute | solution.py:491
  59.3 3.3 %collective-permute-done.12 = f32[88,256]{1,0:T(8,128)S(1)} collective-permute-done((f32[88,256]{1,0:T(8,128)S(1)}, f32[88,256]{1,0:T(8,128)S(1)}, u32[]{:S(2)}, u32[]{:S(2)}) %collective-permute-start.12) | collective-permute-done | bytes 90144 | tf_op jit(solution)/shard_map/ppermute | solution.py:491
  62.7 0.1 broadcast_in_dim.19
  62.8 23.7 %all_to_all.5.pieces_ref = f32[16,88,256]{2,1,0:T(8,128)S(1)} all-to-all(f32[16,88,256]{2,1,0:T(8,128)S(1)} %broadcast_in_dim.19), channel_id=1, replica_groups={{0,1,2,3,4,5,6,7,8,9,10,11,12,13,14,15},{16,17,18,19,20,21,22,23,24,25,..., dimensions={0} | all-to-all | bytes 2883584 | tf_op jit(solution)/shard_map/all_to_all | solution.py:520
  86.4 1.7 %weight_rows.1 = (f32[16,80,256]{2,1,0:T(8,128)}, f32[1,20]{1,0:T(1,128)}, f32[1,20]{1,0:T(1,128)}) custom-call(f32[16,88,256]{2,1,0:T(8,128)S(1)} %all_to_all.5.pieces_ref), custom_call_target="tpu_custom_call" | custom-call | flops 10000 | bytes 2600000 | tf_op jit(solution)/shard_map/weight_rows/pallas_call | solution.py:457
  (7 shorter events, 0.1 us)
Async XLA Ops:
  1.3 0.8 copy-start.5
  2.1 0.7 copy-start.7
  2.7 6.0 %copy-start.1 = (bf16[1,256,2560]{2,1,0:T(8,128)(2,1)S(1)}, bf16[1,256,2560]{2,1,0:T(8,128)(2,1)}, u32[]{:S(2)}) copy-start(bf16[1,256,2560]{2,1,0:T(8,128)(2,1)} %param.9) | copy-start | bytes 3932164
  2.7 6.0 %copy-start.3 = (bf16[1,256,2560]{2,1,0:T(8,128)(2,1)S(1)}, bf16[1,256,2560]{2,1,0:T(8,128)(2,1)}, u32[]{:S(2)}) copy-start(bf16[1,256,2560]{2,1,0:T(8,128)(2,1)} %param.10) | copy-start | bytes 3932164
  8.1 3.6 %copy-start.8 = (f32[5,256,8]{2,1,0:T(8,128)}, f32[5,256,8]{2,1,0:T(8,128)S(1)}, u32[]{:S(2)}) copy-start(f32[5,256,8]{2,1,0:T(8,128)S(1)} %get-tuple-element.29.cols_ref) | copy-start | bytes 122884
  8.1 4.0 %collective-permute-start = (f32[128,2560]{1,0:T(8,128)S(1)}, f32[128,2560]{1,0:T(8,128)S(1)}, u32[]{:S(2)}, u32[]{:S(2)}) collective-permute-start(f32[128,2560]{1,0:T(8,128)S(1)} %get-tuple-element.32), channel_id=1, source_target_pairs={{0,128},{128,0},{1,129},{129,1},{2,130},{130,2},{3,131},{131,3},{4... | collective-permute-start | bytes 3932168 | tf_op jit(solution)/shard_map/ppermute | solution.py:495
  8.2 5.2 %collective-permute-start.2 = (f32[256,1280]{1,0:T(8,128)}, f32[256,1280]{1,0:T(8,128)}, u32[]{:S(2)}, u32[]{:S(2)}) collective-permute-start(f32[256,1280]{1,0:T(8,128)} %get-tuple-element.38), channel_id=1, source_target_pairs={{0,128},{128,0},{1,129},{129,1},{2,130},{130,2},{3,131},{131,3},{4... | collective-permute-start | bytes 3932168 | tf_op jit(solution)/shard_map/ppermute | solution.py:495
  12.1 2.7 %copy-start = (bf16[1,256,2560]{2,1,0:T(8,128)(2,1)S(1)}, bf16[1,256,2560]{2,1,0:T(8,128)(2,1)}, u32[]{:S(2)}) copy-start(bf16[1,256,2560]{2,1,0:T(8,128)(2,1)} %param.8) | copy-start | bytes 3932164
  13.2 1.6 %collective-permute-start.1 = (f32[256,256]{1,0:T(8,128)S(1)}, f32[256,256]{1,0:T(8,128)S(1)}, u32[]{:S(2)}, u32[]{:S(2)}) collective-permute-start(f32[256,256]{1,0:T(8,128)S(1)} %proj_gradient.1.grad_ref), channel_id=1, source_target_pairs={{0,128},{128,0},{1,129},{129,1},{2,130},{130,2},{3,131},{131,3},{4... | collective-permute-start | bytes 786440 | tf_op jit(solution)/shard_map/ppermute | solution.py:495
  13.4 9.5 %copy-start.2 = (bf16[1,256,2560]{2,1,0:T(8,128)(2,1)S(1)}, bf16[1,256,2560]{2,1,0:T(8,128)(2,1)}, u32[]{:S(2)}) copy-start(bf16[1,256,2560]{2,1,0:T(8,128)(2,1)} %param.9) | copy-start | bytes 3932164
  13.4 9.5 %copy-start.4 = (bf16[1,256,2560]{2,1,0:T(8,128)(2,1)S(1)}, bf16[1,256,2560]{2,1,0:T(8,128)(2,1)}, u32[]{:S(2)}) copy-start(bf16[1,256,2560]{2,1,0:T(8,128)(2,1)} %param.10) | copy-start | bytes 3932164
  13.4 9.5 %copy-start.6 = (f32[1,40,256]{2,1,0:T(8,128)S(1)}, f32[1,40,256]{2,1,0:T(8,128)}, u32[]{:S(2)}) copy-start(f32[1,40,256]{2,1,0:T(8,128)} %param.11) | copy-start | bytes 122884
  13.4 9.5 %copy-start.9 = (f32[5,256,8]{2,1,0:T(8,128)S(1)}, f32[5,256,8]{2,1,0:T(8,128)}, u32[]{:S(2)}) copy-start(f32[5,256,8]{2,1,0:T(8,128)} %copy-done.8) | copy-start | bytes 122884
  13.4 9.5 %copy-start.10 = (f32[40]{0:T(128)S(1)}, f32[40]{0:T(128)}, u32[]{:S(2)}) copy-start(f32[40]{0:T(128)} %param.14) | copy-start | bytes 484
  17.1 15.7 %collective-permute-start.3 = (f32[320,256]{1,0:T(8,128)S(1)}, f32[320,256]{1,0:T(8,128)S(1)}, u32[]{:S(2)}, u32[]{:S(2)}) collective-permute-start(f32[320,256]{1,0:T(8,128)S(1)} %get-tuple-element.40), channel_id=1, source_target_pairs={{0,1},{1,2},{2,3},{3,0},{4,5},{5,6},{6,7},{7,4},{8,9},{9,10},{10,1... | collective-permute-start | bytes 983048 | tf_op jit(solution)/shard_map/ppermute | solution.py:487
  18.7 14.2 %collective-permute-start.4 = (f32[320,256]{1,0:T(8,128)S(1)}, f32[320,256]{1,0:T(8,128)S(1)}, u32[]{:S(2)}, u32[]{:S(2)}) collective-permute-start(f32[320,256]{1,0:T(8,128)S(1)} %get-tuple-element.41), channel_id=1, source_target_pairs={{0,2},{1,3},{2,0},{3,1},{4,6},{5,7},{6,4},{7,5},{8,10},{9,11},{10,... | collective-permute-start | bytes 983048 | tf_op jit(solution)/shard_map/ppermute | solution.py:487
  21.4 11.4 %collective-permute-start.5 = (f32[320,256]{1,0:T(8,128)S(1)}, f32[320,256]{1,0:T(8,128)S(1)}, u32[]{:S(2)}, u32[]{:S(2)}) collective-permute-start(f32[320,256]{1,0:T(8,128)S(1)} %get-tuple-element.42), channel_id=1, source_target_pairs={{0,3},{1,0},{2,1},{3,2},{4,7},{5,4},{6,5},{7,6},{8,11},{9,8},{10,9... | collective-permute-start | bytes 983048 | tf_op jit(solution)/shard_map/ppermute | solution.py:487
  33.0 6.5 %collective-permute-start.8 = (f32[80,256]{1,0:T(8,128)S(1)}, f32[80,256]{1,0:T(8,128)S(1)}, u32[]{:S(2)}, u32[]{:S(2)}) collective-permute-start(f32[80,256]{1,0:T(8,128)S(1)} %get-tuple-element.52), channel_id=1, source_target_pairs={{0,12},{1,13},{2,14},{3,15},{4,0},{5,1},{6,2},{7,3},{8,4},{9,5},{1... | collective-permute-start | bytes 245768 | tf_op jit(solution)/shard_map/ppermute | solution.py:487
  36.1 6.5 %collective-permute-start.6 = (f32[80,256]{1,0:T(8,128)S(1)}, f32[80,256]{1,0:T(8,128)S(1)}, u32[]{:S(2)}, u32[]{:S(2)}) collective-permute-start(f32[80,256]{1,0:T(8,128)S(1)} %get-tuple-element.53), channel_id=1, source_target_pairs={{0,4},{1,5},{2,6},{3,7},{4,8},{5,9},{6,10},{7,11},{8,12},{9,13},{1... | collective-permute-start | bytes 245768 | tf_op jit(solution)/shard_map/ppermute | solution.py:487
  36.1 6.5 %collective-permute-start.7 = (f32[80,256]{1,0:T(8,128)S(1)}, f32[80,256]{1,0:T(8,128)S(1)}, u32[]{:S(2)}, u32[]{:S(2)}) collective-permute-start(f32[80,256]{1,0:T(8,128)S(1)} %get-tuple-element.51), channel_id=1, source_target_pairs={{0,8},{1,9},{2,10},{3,11},{4,12},{5,13},{6,14},{7,15},{8,0},{9,1},... | collective-permute-start | bytes 245768 | tf_op jit(solution)/shard_map/ppermute | solution.py:487
  38.3 1.2 %collective-permute-start.9 = (f32[8,256]{1,0:T(8,128)S(1)}, f32[8,256]{1,0:T(8,128)S(1)}, u32[]{:S(2)}, u32[]{:S(2)}) collective-permute-start(f32[8,256]{1,0:T(8,128)S(1)} %get-tuple-element.47), channel_id=1, source_target_pairs={{0,128},{128,0},{1,129},{129,1},{2,130},{130,2},{3,131},{131,3},{4... | collective-permute-start | bytes 24584 | tf_op jit(solution)/shard_map/ppermute | solution.py:495
  42.7 4.6 %collective-permute-start.10 = (f32[88,256]{1,0:T(8,128)S(1)}, f32[88,256]{1,0:T(8,128)S(1)}, u32[]{:S(2)}, u32[]{:S(2)}) collective-permute-start(f32[88,256]{1,0:T(8,128)S(1)} %pad_maximum_fusion), channel_id=1, source_target_pairs={{0,16},{1,17},{2,18},{3,19},{4,20},{5,21},{6,22},{7,23},{8,24},{9,... | collective-permute-start | bytes 270344 | tf_op jit(solution)/shard_map/ppermute | solution.py:491
  47.3 6.4 %collective-permute-start.11 = (f32[88,256]{1,0:T(8,128)S(1)}, f32[88,256]{1,0:T(8,128)S(1)}, u32[]{:S(2)}, u32[]{:S(2)}) collective-permute-start(f32[88,256]{1,0:T(8,128)S(1)} %fusion), channel_id=1, source_target_pairs={{0,32},{1,33},{2,34},{3,35},{4,36},{5,37},{6,38},{7,39},{8,40},{9,... | collective-permute-start | bytes 270344 | tf_op jit(solution)/shard_map/ppermute | solution.py:491
  53.7 8.9 %collective-permute-start.12 = (f32[88,256]{1,0:T(8,128)S(1)}, f32[88,256]{1,0:T(8,128)S(1)}, u32[]{:S(2)}, u32[]{:S(2)}) collective-permute-start(f32[88,256]{1,0:T(8,128)S(1)} %add.92), channel_id=1, source_target_pairs={{0,96},{1,97},{2,98},{3,99},{4,100},{5,101},{6,102},{7,103},{8,104... | collective-permute-start | bytes 270344 | tf_op jit(solution)/shard_map/ppermute | solution.py:491

commit v3 on v2

--- a/solution.py
+++ b/solution.py
@@ -508,9 +508,10 @@
     _, second = ring_place()
     sent = [ring_shift(pieces[k], 0, k) for k in range(1, RING)]
     dx, dstep, small = input_call(tile_list, x, g, run, cols, scale, step, rates, skip_gain[None], state, proj)
-    sent, small = lax.optimization_barrier((sent, small))
-    small = small + swap(small)
+    small_own = small
     part = pieces[0] + sent[0] + sent[1] + sent[2]
+    part, small_own = lax.optimization_barrier((part, small_own))
+    small = small_own + swap(small_own)
     cut = [lax.dynamic_slice_in_dim(part, (second + k) % RING * ROWS, ROWS, 0) for k in range(RING)]
     part = cut[0] + sum(ring_shift(cut[k], 1, k) for k in range(1, RING))
     part = jnp.concatenate([part, small], axis=0)

time: 88.5 us -> 85 us (0.960)
  blocking collectives: 23.7 us -> 20.6 us
    all_to_all x1, blocking collectives: 23.7 us -> 20.6 us  [shards(): lax.all_to_all(jnp.broadcast_to(part, (PLANE,) + part.shape), 'dp', 0, 0,...]
    ppermute x6, starting transfers between devices: 11 us -> 9.83 us  [ring_shift(): return lax.ppermute(v, ('seq', 'dp'), pairs)]
  transfers between devices with their start and end apart: 13 -> 13, of which waited for: 7 -> 8; matrix products, arithmetic and copies ran while one was open for 0% -> 0% of each run, Pallas kernels for 16% -> 16%
where the time goes in v3:
time: 85 us; the launch traced here: 84.8 us
  Pallas kernels  23.4 us (28%)
  blocking collectives  20.6 us (24%)
  starting transfers between devices  20.3 us (24%)
  waiting for transfers between devices  17.1 us (20%)
  local copies, waits for them, and re-layouts  1.59 us (2%)
  between operations  1.59 us (2%)
    all_to_all x1, blocking collectives, shards(): lax.all_to_all(jnp.broadcast_to(part, (PLANE,) + part.shape), 'dp', 0, 0,...  20.6 us
    ppermute x3, waiting for transfers between devices, across_z(): lax.ppermute(v, 'dp', [(i, moved(i, 'z', 8, lambda c: c ^ bit)) for i in...  10.6 us
    pallas_call x1, Pallas kernels, input_call(): pl.pallas_call(input_kernel, name='input_gradient', grid=(GROUPS,), out_s...  9.95 us
    ppermute x6, starting transfers between devices, ring_shift(): return lax.ppermute(v, ('seq', 'dp'), pairs)  9.83 us
    ppermute x3, starting transfers between devices, across_z(): lax.ppermute(v, 'dp', [(i, moved(i, 'z', 8, lambda c: c ^ bit)) for i in...  9.68 us
    pallas_call x1, Pallas kernels, state_call(): pl.pallas_call(state_kernel, name='state_to_send', out_shape=(jax.ShapeDt...  5.38 us
    ppermute x6, waiting for transfers between devices, ring_shift(): return lax.ppermute(v, ('seq', 'dp'), pairs)  3.57 us
    ppermute x4, waiting for transfers between devices, swap(): return lax.ppermute(v, 'seq', [(0, 1), (1, 0)])  2.97 us
  transfers between devices with their start and end apart: 13, of which 8 were waited for; matrix products, arithmetic and copies ran while one was open for 0% of the time, Pallas kernels for 16%

profile of v3, /device:TPU:32, one launch (start us, length us, event | category | flops | bytes accessed | tf_op | source)
XLA Modules:
  0.0 84.8 jit_solution(17068821121443941055)
XLA Ops:
  1.3 0.0 copy-start.5
  1.3 0.8 copy-done.5
  2.1 0.0 copy-start.7
  2.1 0.7 copy-done.7
  2.7 0.0 copy-start.1
  2.7 0.0 copy-start.3
  2.7 5.4 %state_to_send.1 = (f32[256,256]{1,0:T(8,128)S(1)}, f32[40,256]{1,0:T(8,128)S(1)}, f32[5,256,8]{2,1,0:T(8,128)S(1)}, f32[40,256]{1,0:T(8,128)S(1)}, f32[40,128]{...) custom-call(s32[1,1]{1,0:T(1,128)S(6)} %copy.13.tile_ref, ...), custom_call_target="tpu_custom_call" | custom-call | flops 1000000000 | bytes 8000000 | tf_op jit(solution)/shard_map/state_to_send/pallas_call | solution.py:156
  8.1 0.0 copy-start.8
  8.1 0.1 collective-permute-start
  8.2 0.5 collective-permute-start.2
  8.7 0.0 copy-done.1
  8.7 0.0 copy-done.3
  8.7 2.9 %score_gradient.1.pair_ref = f32[256,256]{1,0:T(8,128)S(1)} custom-call(bf16[256,2560]{1,0:T(8,128)(2,1)S(1)} %bitcast.14, bf16[256,2560]{1,0:T(8,128)(2,1)S(1)} %bitcast.17, f32[40,256]{1,0:T(8,128)S(1)} %get-tuple-element.26.run_ref, f32[5,256,8]{2,1,0:T(8,128)S(1)} %get-tuple-element.27.cols_ref), custom_call_target="tpu_custom_call" | custom-call | flops 1500000000 | bytes 3000000 | tf_op jit(solution)/shard_map/score_gradient/pallas_call | solution.py:226
  11.7 0.0 copy-done.8
  11.7 0.4 collective-permute-done.state_ref
  12.1 0.0 copy-start
  12.1 1.0 %proj_gradient.1.grad_ref = f32[256,256]{1,0:T(8,128)S(1)} custom-call(s32[1,1]{1,0:T(1,128)S(6)} %copy.13.tile_ref, f32[256,256]{1,0:T(8,128)S(1)} %score_gradient.1.pair_ref, f32[256,256]{1,0:T(8,128)S(1)} %get-tuple-element.31.proj_ref, bf16[256,2560]{1,0:T(8,128)(2,1)S(1)} %get-tuple-element.34.high_ref, ...), custom_call_target="tpu_custom_call" | custom-call | flops 700000000 | bytes 4000000 | tf_op jit(solution)/shard_map/proj_gradient/pallas_call | solution.py:260
  13.2 0.2 collective-permute-start.1
  13.4 0.0 copy-start.2
  13.4 0.0 copy-start.4
  13.4 0.0 copy-start.6
  13.4 0.0 copy-start.9
  13.4 0.0 copy-start.10
  13.4 0.0 collective-permute-done.2.wide_ref
  13.5 1.3 %collective-permute-done.1.other_ref = f32[256,256]{1,0:T(8,128)S(1)} collective-permute-done((f32[256,256]{1,0:T(8,128)S(1)}, f32[256,256]{1,0:T(8,128)S(1)}, u32[]{:S(2)}, u32[]{:S(2)}) %collective-permute-start.1) | collective-permute-done | bytes 262176 | tf_op jit(solution)/shard_map/ppermute | solution.py:495
  14.8 0.0 copy-done
  14.8 2.4 %weight_gradient.1 = (f32[320,256]{1,0:T(8,128)S(1)}, f32[320,256]{1,0:T(8,128)S(1)}, f32[320,256]{1,0:T(8,128)S(1)}, f32[320,256]{1,0:T(8,128)S(1)}) custom-call(f32[256,256]{1,0:T(8,128)S(1)} %proj_gradient.1.grad_ref, f32[256,256]{1,0:T(8,128)S(1)} %collective-permute-done.1.other_ref, bf16[256,2560]{1,0:T(8,128)(2,1)S(1)} %bitcast.12, ...), custom_call_target="tpu_custom_call" | custom-call | flops 1400000000 | bytes 4000000 | tf_op jit(solution)/shard_map/weight_gradient/pallas_call | solution.py:297
  17.1 2.8 %collective-permute-start.5 = (f32[320,256]{1,0:T(8,128)S(1)}, f32[320,256]{1,0:T(8,128)S(1)}, u32[]{:S(2)}, u32[]{:S(2)}) collective-permute-start(f32[320,256]{1,0:T(8,128)S(1)} %get-tuple-element.40), channel_id=1, source_target_pairs={{0,3},{1,0},{2,1},{3,2},{4,7},{5,4},{6,5},{7,6},{8,11},{9,8},{10,9... | collective-permute-start | bytes 983048 | tf_op jit(solution)/shard_map/ppermute | solution.py:487
  20.0 0.8 collective-permute-start.4
  20.8 0.9 %collective-permute-start.3 = (f32[320,256]{1,0:T(8,128)S(1)}, f32[320,256]{1,0:T(8,128)S(1)}, u32[]{:S(2)}, u32[]{:S(2)}) collective-permute-start(f32[320,256]{1,0:T(8,128)S(1)} %get-tuple-element.38), channel_id=1, source_target_pairs={{0,1},{1,2},{2,3},{3,0},{4,5},{5,6},{6,7},{7,4},{8,9},{9,10},{10,1... | collective-permute-start | bytes 983048 | tf_op jit(solution)/shard_map/ppermute | solution.py:487
  21.7 0.0 copy-done.2
  21.7 0.0 copy-done.4
  21.7 0.0 copy-done.6
  21.7 0.0 copy-done.9
  21.7 0.0 copy-done.10
  21.7 9.9 %input_gradient.1 = (bf16[256,2560]{1,0:T(8,128)(2,1)}, f32[40,256]{1,0:T(8,128)}, f32[8,256]{1,0:T(8,128)S(1)}) custom-call(s32[1,1]{1,0:T(1,128)S(6)} %copy.13.tile_ref, bf16[256,2560]{1,0:T(8,128)(2,1)S(1)} %bitcast.15, bf16[256,2560]{1,0:T(8,128)(2,1)S(1)} %bitcast.18, f32[40,256]{1,0:T(8,128)S(1)} %get-tuple-element.26.run_ref, ...), custom_call_target="tpu_custom_call" | custom-call | flops 6000000000 | bytes 8000000 | tf_op jit(solution)/shard_map/input_gradient/pallas_call | solution.py:397
  31.7 0.0 collective-permute-done.5
  31.7 0.0 collective-permute-done.4
  31.7 0.4 collective-permute-done.3
  32.1 0.1 add_add_fusion
  32.2 3.1 %collective-permute-start.8 = (f32[80,256]{1,0:T(8,128)S(1)}, f32[80,256]{1,0:T(8,128)S(1)}, u32[]{:S(2)}, u32[]{:S(2)}) collective-permute-start(f32[80,256]{1,0:T(8,128)S(1)} %get-tuple-element.48), channel_id=1, source_target_pairs={{0,12},{1,13},{2,14},{3,15},{4,0},{5,1},{6,2},{7,3},{8,4},{9,5},{1... | collective-permute-start | bytes 245768 | tf_op jit(solution)/shard_map/ppermute | solution.py:487
  35.3 0.0 collective-permute-start.6
  35.3 2.2 %collective-permute-start.7 = (f32[80,256]{1,0:T(8,128)S(1)}, f32[80,256]{1,0:T(8,128)S(1)}, u32[]{:S(2)}, u32[]{:S(2)}) collective-permute-start(f32[80,256]{1,0:T(8,128)S(1)} %get-tuple-element.47), channel_id=1, source_target_pairs={{0,8},{1,9},{2,10},{3,11},{4,12},{5,13},{6,14},{7,15},{8,0},{9,1},... | collective-permute-start | bytes 245768 | tf_op jit(solution)/shard_map/ppermute | solution.py:487
  37.5 0.0 collective-permute-start.9
  37.5 1.2 %collective-permute-done.9 = f32[8,256]{1,0:T(8,128)S(1)} collective-permute-done((f32[8,256]{1,0:T(8,128)S(1)}, f32[8,256]{1,0:T(8,128)S(1)}, u32[]{:S(2)}, u32[]{:S(2)}) %collective-permute-start.9) | collective-permute-done | bytes 8224 | tf_op jit(solution)/shard_map/ppermute | solution.py:495
  38.7 0.0 collective-permute-done.8
  38.7 3.1 %collective-permute-done.6 = f32[80,256]{1,0:T(8,128)S(1)} collective-permute-done((f32[80,256]{1,0:T(8,128)S(1)}, f32[80,256]{1,0:T(8,128)S(1)}, u32[]{:S(2)}, u32[]{:S(2)}) %collective-permute-start.6) | collective-permute-done | bytes 81952 | tf_op jit(solution)/shard_map/ppermute | solution.py:487
  41.8 0.0 collective-permute-done.7
  41.9 0.2 collective-permute-start.10
  42.1 4.4 %collective-permute-done.10 = f32[88,256]{1,0:T(8,128)S(1)} collective-permute-done((f32[88,256]{1,0:T(8,128)S(1)}, f32[88,256]{1,0:T(8,128)S(1)}, u32[]{:S(2)}, u32[]{:S(2)}) %collective-permute-start.10) | collective-permute-done | bytes 90144 | tf_op jit(solution)/shard_map/ppermute | solution.py:491
  46.5 3.4 %collective-permute-start.11 = (f32[88,256]{1,0:T(8,128)S(1)}, f32[88,256]{1,0:T(8,128)S(1)}, u32[]{:S(2)}, u32[]{:S(2)}) collective-permute-start(f32[88,256]{1,0:T(8,128)S(1)} %fusion), channel_id=1, source_target_pairs={{0,32},{1,33},{2,34},{3,35},{4,36},{5,37},{6,38},{7,39},{8,40},{9,... | collective-permute-start | bytes 270344 | tf_op jit(solution)/shard_map/ppermute | solution.py:491
  49.9 3.0 %collective-permute-done.11 = f32[88,256]{1,0:T(8,128)S(1)} collective-permute-done((f32[88,256]{1,0:T(8,128)S(1)}, f32[88,256]{1,0:T(8,128)S(1)}, u32[]{:S(2)}, u32[]{:S(2)}) %collective-permute-start.11) | collective-permute-done | bytes 90144 | tf_op jit(solution)/shard_map/ppermute | solution.py:491
  53.0 6.1 %collective-permute-start.12 = (f32[88,256]{1,0:T(8,128)S(1)}, f32[88,256]{1,0:T(8,128)S(1)}, u32[]{:S(2)}, u32[]{:S(2)}) collective-permute-start(f32[88,256]{1,0:T(8,128)S(1)} %add.92), channel_id=1, source_target_pairs={{0,96},{1,97},{2,98},{3,99},{4,100},{5,101},{6,102},{7,103},{8,104... | collective-permute-start | bytes 270344 | tf_op jit(solution)/shard_map/ppermute | solution.py:491
  59.1 3.1 %collective-permute-done.12 = f32[88,256]{1,0:T(8,128)S(1)} collective-permute-done((f32[88,256]{1,0:T(8,128)S(1)}, f32[88,256]{1,0:T(8,128)S(1)}, u32[]{:S(2)}, u32[]{:S(2)}) %collective-permute-start.12) | collective-permute-done | bytes 90144 | tf_op jit(solution)/shard_map/ppermute | solution.py:491
  62.2 0.1 broadcast_in_dim.19
  62.3 20.6 %all_to_all.5.pieces_ref = f32[16,88,256]{2,1,0:T(8,128)S(1)} all-to-all(f32[16,88,256]{2,1,0:T(8,128)S(1)} %broadcast_in_dim.19), channel_id=1, replica_groups={{0,1,2,3,4,5,6,7,8,9,10,11,12,13,14,15},{16,17,18,19,20,21,22,23,24,25,..., dimensions={0} | all-to-all | bytes 2883584 | tf_op jit(solution)/shard_map/all_to_all | solution.py:521
  82.9 1.7 %weight_rows.1 = (f32[16,80,256]{2,1,0:T(8,128)}, f32[1,20]{1,0:T(1,128)}, f32[1,20]{1,0:T(1,128)}) custom-call(f32[16,88,256]{2,1,0:T(8,128)S(1)} %all_to_all.5.pieces_ref), custom_call_target="tpu_custom_call" | custom-call | flops 10000 | bytes 2600000 | tf_op jit(solution)/shard_map/weight_rows/pallas_call | solution.py:457
  (7 shorter events, 0.1 us)
Async XLA Ops:
  1.3 0.8 copy-start.5
  2.1 0.7 copy-start.7
  2.7 6.0 %copy-start.1 = (bf16[1,256,2560]{2,1,0:T(8,128)(2,1)S(1)}, bf16[1,256,2560]{2,1,0:T(8,128)(2,1)}, u32[]{:S(2)}) copy-start(bf16[1,256,2560]{2,1,0:T(8,128)(2,1)} %param.9) | copy-start | bytes 3932164
  2.7 6.0 %copy-start.3 = (bf16[1,256,2560]{2,1,0:T(8,128)(2,1)S(1)}, bf16[1,256,2560]{2,1,0:T(8,128)(2,1)}, u32[]{:S(2)}) copy-start(bf16[1,256,2560]{2,1,0:T(8,128)(2,1)} %param.10) | copy-start | bytes 3932164
  8.1 3.6 %copy-start.8 = (f32[5,256,8]{2,1,0:T(8,128)}, f32[5,256,8]{2,1,0:T(8,128)S(1)}, u32[]{:S(2)}) copy-start(f32[5,256,8]{2,1,0:T(8,128)S(1)} %get-tuple-element.27.cols_ref) | copy-start | bytes 122884
  8.1 4.0 %collective-permute-start = (f32[128,2560]{1,0:T(8,128)S(1)}, f32[128,2560]{1,0:T(8,128)S(1)}, u32[]{:S(2)}, u32[]{:S(2)}) collective-permute-start(f32[128,2560]{1,0:T(8,128)S(1)} %get-tuple-element.30), channel_id=1, source_target_pairs={{0,128},{128,0},{1,129},{129,1},{2,130},{130,2},{3,131},{131,3},{4... | collective-permute-start | bytes 3932168 | tf_op jit(solution)/shard_map/ppermute | solution.py:495
  8.2 5.2 %collective-permute-start.2 = (f32[256,1280]{1,0:T(8,128)}, f32[256,1280]{1,0:T(8,128)}, u32[]{:S(2)}, u32[]{:S(2)}) collective-permute-start(f32[256,1280]{1,0:T(8,128)} %get-tuple-element.36), channel_id=1, source_target_pairs={{0,128},{128,0},{1,129},{129,1},{2,130},{130,2},{3,131},{131,3},{4... | collective-permute-start | bytes 3932168 | tf_op jit(solution)/shard_map/ppermute | solution.py:495
  12.1 2.7 %copy-start = (bf16[1,256,2560]{2,1,0:T(8,128)(2,1)S(1)}, bf16[1,256,2560]{2,1,0:T(8,128)(2,1)}, u32[]{:S(2)}) copy-start(bf16[1,256,2560]{2,1,0:T(8,128)(2,1)} %param.8) | copy-start | bytes 3932164
  13.2 1.6 %collective-permute-start.1 = (f32[256,256]{1,0:T(8,128)S(1)}, f32[256,256]{1,0:T(8,128)S(1)}, u32[]{:S(2)}, u32[]{:S(2)}) collective-permute-start(f32[256,256]{1,0:T(8,128)S(1)} %proj_gradient.1.grad_ref), channel_id=1, source_target_pairs={{0,128},{128,0},{1,129},{129,1},{2,130},{130,2},{3,131},{131,3},{4... | collective-permute-start | bytes 786440 | tf_op jit(solution)/shard_map/ppermute | solution.py:495
  13.4 8.3 %copy-start.2 = (bf16[1,256,2560]{2,1,0:T(8,128)(2,1)S(1)}, bf16[1,256,2560]{2,1,0:T(8,128)(2,1)}, u32[]{:S(2)}) copy-start(bf16[1,256,2560]{2,1,0:T(8,128)(2,1)} %param.9) | copy-start | bytes 3932164
  13.4 8.3 %copy-start.4 = (bf16[1,256,2560]{2,1,0:T(8,128)(2,1)S(1)}, bf16[1,256,2560]{2,1,0:T(8,128)(2,1)}, u32[]{:S(2)}) copy-start(bf16[1,256,2560]{2,1,0:T(8,128)(2,1)} %param.10) | copy-start | bytes 3932164
  13.4 8.3 %copy-start.6 = (f32[1,40,256]{2,1,0:T(8,128)S(1)}, f32[1,40,256]{2,1,0:T(8,128)}, u32[]{:S(2)}) copy-start(f32[1,40,256]{2,1,0:T(8,128)} %param.11) | copy-start | bytes 122884
  13.4 8.3 %copy-start.9 = (f32[5,256,8]{2,1,0:T(8,128)S(1)}, f32[5,256,8]{2,1,0:T(8,128)}, u32[]{:S(2)}) copy-start(f32[5,256,8]{2,1,0:T(8,128)} %copy-done.8) | copy-start | bytes 122884
  13.4 8.3 %copy-start.10 = (f32[40]{0:T(128)S(1)}, f32[40]{0:T(128)}, u32[]{:S(2)}) copy-start(f32[40]{0:T(128)} %param.14) | copy-start | bytes 484
  17.1 14.5 %collective-permute-start.5 = (f32[320,256]{1,0:T(8,128)S(1)}, f32[320,256]{1,0:T(8,128)S(1)}, u32[]{:S(2)}, u32[]{:S(2)}) collective-permute-start(f32[320,256]{1,0:T(8,128)S(1)} %get-tuple-element.40), channel_id=1, source_target_pairs={{0,3},{1,0},{2,1},{3,2},{4,7},{5,4},{6,5},{7,6},{8,11},{9,8},{10,9... | collective-permute-start | bytes 983048 | tf_op jit(solution)/shard_map/ppermute | solution.py:487
  20.0 11.7 %collective-permute-start.4 = (f32[320,256]{1,0:T(8,128)S(1)}, f32[320,256]{1,0:T(8,128)S(1)}, u32[]{:S(2)}, u32[]{:S(2)}) collective-permute-start(f32[320,256]{1,0:T(8,128)S(1)} %get-tuple-element.39), channel_id=1, source_target_pairs={{0,2},{1,3},{2,0},{3,1},{4,6},{5,7},{6,4},{7,5},{8,10},{9,11},{10,... | collective-permute-start | bytes 983048 | tf_op jit(solution)/shard_map/ppermute | solution.py:487
  20.8 11.3 %collective-permute-start.3 = (f32[320,256]{1,0:T(8,128)S(1)}, f32[320,256]{1,0:T(8,128)S(1)}, u32[]{:S(2)}, u32[]{:S(2)}) collective-permute-start(f32[320,256]{1,0:T(8,128)S(1)} %get-tuple-element.38), channel_id=1, source_target_pairs={{0,1},{1,2},{2,3},{3,0},{4,5},{5,6},{6,7},{7,4},{8,9},{9,10},{10,1... | collective-permute-start | bytes 983048 | tf_op jit(solution)/shard_map/ppermute | solution.py:487
  32.2 6.5 %collective-permute-start.8 = (f32[80,256]{1,0:T(8,128)S(1)}, f32[80,256]{1,0:T(8,128)S(1)}, u32[]{:S(2)}, u32[]{:S(2)}) collective-permute-start(f32[80,256]{1,0:T(8,128)S(1)} %get-tuple-element.48), channel_id=1, source_target_pairs={{0,12},{1,13},{2,14},{3,15},{4,0},{5,1},{6,2},{7,3},{8,4},{9,5},{1... | collective-permute-start | bytes 245768 | tf_op jit(solution)/shard_map/ppermute | solution.py:487
  35.3 6.5 %collective-permute-start.6 = (f32[80,256]{1,0:T(8,128)S(1)}, f32[80,256]{1,0:T(8,128)S(1)}, u32[]{:S(2)}, u32[]{:S(2)}) collective-permute-start(f32[80,256]{1,0:T(8,128)S(1)} %get-tuple-element.49), channel_id=1, source_target_pairs={{0,4},{1,5},{2,6},{3,7},{4,8},{5,9},{6,10},{7,11},{8,12},{9,13},{1... | collective-permute-start | bytes 245768 | tf_op jit(solution)/shard_map/ppermute | solution.py:487
  35.3 6.5 %collective-permute-start.7 = (f32[80,256]{1,0:T(8,128)S(1)}, f32[80,256]{1,0:T(8,128)S(1)}, u32[]{:S(2)}, u32[]{:S(2)}) collective-permute-start(f32[80,256]{1,0:T(8,128)S(1)} %get-tuple-element.47), channel_id=1, source_target_pairs={{0,8},{1,9},{2,10},{3,11},{4,12},{5,13},{6,14},{7,15},{8,0},{9,1},... | collective-permute-start | bytes 245768 | tf_op jit(solution)/shard_map/ppermute | solution.py:487
  37.5 1.2 %collective-permute-start.9 = (f32[8,256]{1,0:T(8,128)S(1)}, f32[8,256]{1,0:T(8,128)S(1)}, u32[]{:S(2)}, u32[]{:S(2)}) collective-permute-start(f32[8,256]{1,0:T(8,128)S(1)} %get-tuple-element.43), channel_id=1, source_target_pairs={{0,128},{128,0},{1,129},{129,1},{2,130},{130,2},{3,131},{131,3},{4... | collective-permute-start | bytes 24584 | tf_op jit(solution)/shard_map/ppermute | solution.py:495
  41.9 4.6 %collective-permute-start.10 = (f32[88,256]{1,0:T(8,128)S(1)}, f32[88,256]{1,0:T(8,128)S(1)}, u32[]{:S(2)}, u32[]{:S(2)}) collective-permute-start(f32[88,256]{1,0:T(8,128)S(1)} %pad_maximum_fusion), channel_id=1, source_target_pairs={{0,16},{1,17},{2,18},{3,19},{4,20},{5,21},{6,22},{7,23},{8,24},{9,... | collective-permute-start | bytes 270344 | tf_op jit(solution)/shard_map/ppermute | solution.py:491
  46.5 6.4 %collective-permute-start.11 = (f32[88,256]{1,0:T(8,128)S(1)}, f32[88,256]{1,0:T(8,128)S(1)}, u32[]{:S(2)}, u32[]{:S(2)}) collective-permute-start(f32[88,256]{1,0:T(8,128)S(1)} %fusion), channel_id=1, source_target_pairs={{0,32},{1,33},{2,34},{3,35},{4,36},{5,37},{6,38},{7,39},{8,40},{9,... | collective-permute-start | bytes 270344 | tf_op jit(solution)/shard_map/ppermute | solution.py:491
  53.0 9.2 %collective-permute-start.12 = (f32[88,256]{1,0:T(8,128)S(1)}, f32[88,256]{1,0:T(8,128)S(1)}, u32[]{:S(2)}, u32[]{:S(2)}) collective-permute-start(f32[88,256]{1,0:T(8,128)S(1)} %add.92), channel_id=1, source_target_pairs={{0,96},{1,97},{2,98},{3,99},{4,100},{5,101},{6,102},{7,103},{8,104... | collective-permute-start | bytes 270344 | tf_op jit(solution)/shard_map/ppermute | solution.py:491

commit v4 on v3

--- a/solution.py
+++ b/solution.py
@@ -288,8 +288,10 @@
         sums[c * chunk : (c + 1) * chunk, :] = got[:, : 2 * STATE] + got[:, 2 * STATE :]
     me, _ = ring_place()
     for k in range(RING):
-        place = lax.rem(me + k, RING) * PIECE
-        outs[k][...] = sums[pl.ds(pl.multiple_of(place, 8), PIECE), :]
+        to = lax.rem(me + k, RING)
+        for b in range(RING):
+            place = jnp.where(role == 0, b * RING + to, to * RING + b) * ROWS
+            outs[k][b * ROWS : (b + 1) * ROWS, :] = sums[pl.ds(pl.multiple_of(place, 8), ROWS), :]
 
 
 def weight_call(grad, other, hidden, wide):
@@ -434,21 +436,16 @@
 
 def last_kernel(pieces_ref, out_ref, rate_ref, gain_ref, small, sems):
     role = lax.axis_index("seq")
-    few = pltpu.make_async_copy(pieces_ref.at[:, pl.ds(ROWS, 8)], small, sems.at[PLANE])
+    few = pltpu.make_async_copy(pieces_ref.at[:, pl.ds(ROWS, 8)], small, sems.at[0])
     few.start()
-    copies = []
-    for j in range(PLANE):
-        place = jnp.where(role == 0, j % RING * RING + j // RING, j)
-        copies.append(pltpu.make_async_copy(pieces_ref.at[j, pl.ds(0, ROWS)], out_ref.at[place], sems.at[j]))
-    for copy in copies:
-        copy.start()
+    rest = pltpu.make_async_copy(pieces_ref.at[:, pl.ds(0, ROWS)], out_ref, sems.at[1])
+    rest.start()
     few.wait()
     total = jnp.sum(jnp.sum(small[...], axis=0), axis=0, keepdims=True)
     share = HEADS // 2
     rate_ref[...] = jnp.where(role == 0, total[:, :share], total[:, share:HEADS])
     gain_ref[...] = jnp.where(role == 0, total[:, 128 : 128 + share], total[:, 128 + share : 128 + HEADS])
-    for copy in copies:
-        copy.wait()
+    rest.wait()
 
 
 def last_call(pieces):
@@ -464,7 +461,7 @@
         ),
         in_specs=[hbm],
         out_specs=(hbm, vm, vm),
-        scratch_shapes=[pltpu.VMEM((PLANE, 8, 2 * STATE), F32), pltpu.SemaphoreType.DMA((PLANE + 1,))],
+        scratch_shapes=[pltpu.VMEM((PLANE, 8, 2 * STATE), F32), pltpu.SemaphoreType.DMA((2,))],
         compiler_params=pltpu.CompilerParams(vmem_limit_bytes=16 * MIB),
         cost_estimate=pl.CostEstimate(flops=10_000, bytes_accessed=2_600_000, transcendentals=0),
     )(pieces)

time: 85 us -> 84.9 us (level)
  no operation moved by 1% of the time
where the time goes in v4:
time: 84.9 us; the launch traced here: 84.6 us
  Pallas kernels  23.2 us (27%)
  blocking collectives  20.6 us (24%)
  starting transfers between devices  20.3 us (24%)
  waiting for transfers between devices  17.1 us (20%)
  local copies, waits for them, and re-layouts  1.59 us (2%)
  between operations  1.59 us (2%)
    all_to_all x1, blocking collectives, shards(): lax.all_to_all(jnp.broadcast_to(part, (PLANE,) + part.shape), 'dp', 0, 0,...  20.6 us
    ppermute x3, waiting for transfers between devices, across_z(): lax.ppermute(v, 'dp', [(i, moved(i, 'z', 8, lambda c: c ^ bit)) for i in...  10.6 us
    pallas_call x1, Pallas kernels, input_call(): pl.pallas_call(input_kernel, name='input_gradient', grid=(GROUPS,), out_s...  9.95 us
    ppermute x6, starting transfers between devices, ring_shift(): return lax.ppermute(v, ('seq', 'dp'), pairs)  9.83 us
    ppermute x3, starting transfers between devices, across_z(): lax.ppermute(v, 'dp', [(i, moved(i, 'z', 8, lambda c: c ^ bit)) for i in...  9.68 us
    pallas_call x1, Pallas kernels, state_call(): pl.pallas_call(state_kernel, name='state_to_send', out_shape=(jax.ShapeDt...  5.38 us
    ppermute x6, waiting for transfers between devices, ring_shift(): return lax.ppermute(v, ('seq', 'dp'), pairs)  3.57 us
    ppermute x4, waiting for transfers between devices, swap(): return lax.ppermute(v, 'seq', [(0, 1), (1, 0)])  2.97 us
  transfers between devices with their start and end apart: 13, of which 8 were waited for; matrix products, arithmetic and copies ran while one was open for 0% of the time, Pallas kernels for 16%

profile of v4, /device:TPU:32, one launch (start us, length us, event | category | flops | bytes accessed | tf_op | source)
XLA Modules:
  0.0 84.6 jit_solution(3511777128545372434)
XLA Ops:
  1.3 0.0 copy-start.5
  1.3 0.8 copy-done.5
  2.1 0.0 copy-start.7
  2.1 0.7 copy-done.7
  2.7 0.0 copy-start.1
  2.7 0.0 copy-start.3
  2.7 5.4 %state_to_send.1 = (f32[256,256]{1,0:T(8,128)S(1)}, f32[40,256]{1,0:T(8,128)S(1)}, f32[5,256,8]{2,1,0:T(8,128)S(1)}, f32[40,256]{1,0:T(8,128)S(1)}, f32[40,128]{...) custom-call(s32[1,1]{1,0:T(1,128)S(6)} %copy.13.tile_ref, ...), custom_call_target="tpu_custom_call" | custom-call | flops 1000000000 | bytes 8000000 | tf_op jit(solution)/shard_map/state_to_send/pallas_call | solution.py:156
  8.1 0.0 copy-start.8
  8.1 0.1 collective-permute-start
  8.2 0.5 collective-permute-start.2
  8.7 0.0 copy-done.1
  8.7 0.0 copy-done.3
  8.7 2.9 %score_gradient.1.pair_ref = f32[256,256]{1,0:T(8,128)S(1)} custom-call(bf16[256,2560]{1,0:T(8,128)(2,1)S(1)} %bitcast.14, bf16[256,2560]{1,0:T(8,128)(2,1)S(1)} %bitcast.17, f32[40,256]{1,0:T(8,128)S(1)} %get-tuple-element.26.run_ref, f32[5,256,8]{2,1,0:T(8,128)S(1)} %get-tuple-element.27.cols_ref), custom_call_target="tpu_custom_call" | custom-call | flops 1500000000 | bytes 3000000 | tf_op jit(solution)/shard_map/score_gradient/pallas_call | solution.py:226
  11.7 0.0 copy-done.8
  11.7 0.4 collective-permute-done.state_ref
  12.1 0.0 copy-start
  12.1 1.0 %proj_gradient.1.grad_ref = f32[256,256]{1,0:T(8,128)S(1)} custom-call(s32[1,1]{1,0:T(1,128)S(6)} %copy.13.tile_ref, f32[256,256]{1,0:T(8,128)S(1)} %score_gradient.1.pair_ref, f32[256,256]{1,0:T(8,128)S(1)} %get-tuple-element.31.proj_ref, bf16[256,2560]{1,0:T(8,128)(2,1)S(1)} %get-tuple-element.34.high_ref, ...), custom_call_target="tpu_custom_call" | custom-call | flops 700000000 | bytes 4000000 | tf_op jit(solution)/shard_map/proj_gradient/pallas_call | solution.py:260
  13.2 0.2 collective-permute-start.1
  13.4 0.0 copy-start.2
  13.4 0.0 copy-start.4
  13.4 0.0 copy-start.6
  13.4 0.0 copy-start.9
  13.4 0.0 copy-start.10
  13.4 0.0 collective-permute-done.2.wide_ref
  13.5 1.3 %collective-permute-done.1.other_ref = f32[256,256]{1,0:T(8,128)S(1)} collective-permute-done((f32[256,256]{1,0:T(8,128)S(1)}, f32[256,256]{1,0:T(8,128)S(1)}, u32[]{:S(2)}, u32[]{:S(2)}) %collective-permute-start.1) | collective-permute-done | bytes 262176 | tf_op jit(solution)/shard_map/ppermute | solution.py:492
  14.8 0.0 copy-done
  14.8 2.3 %weight_gradient.1 = (f32[320,256]{1,0:T(8,128)S(1)}, f32[320,256]{1,0:T(8,128)S(1)}, f32[320,256]{1,0:T(8,128)S(1)}, f32[320,256]{1,0:T(8,128)S(1)}) custom-call(f32[256,256]{1,0:T(8,128)S(1)} %proj_gradient.1.grad_ref, f32[256,256]{1,0:T(8,128)S(1)} %collective-permute-done.1.other_ref, bf16[256,2560]{1,0:T(8,128)(2,1)S(1)} %bitcast.12, ...), custom_call_target="tpu_custom_call" | custom-call | flops 1400000000 | bytes 4000000 | tf_op jit(solution)/shard_map/weight_gradient/pallas_call | solution.py:299
  17.1 2.8 %collective-permute-start.5 = (f32[320,256]{1,0:T(8,128)S(1)}, f32[320,256]{1,0:T(8,128)S(1)}, u32[]{:S(2)}, u32[]{:S(2)}) collective-permute-start(f32[320,256]{1,0:T(8,128)S(1)} %get-tuple-element.40), channel_id=1, source_target_pairs={{0,3},{1,0},{2,1},{3,2},{4,7},{5,4},{6,5},{7,6},{8,11},{9,8},{10,9... | collective-permute-start | bytes 983048 | tf_op jit(solution)/shard_map/ppermute | solution.py:484
  19.9 0.8 collective-permute-start.4
  20.7 0.9 %collective-permute-start.3 = (f32[320,256]{1,0:T(8,128)S(1)}, f32[320,256]{1,0:T(8,128)S(1)}, u32[]{:S(2)}, u32[]{:S(2)}) collective-permute-start(f32[320,256]{1,0:T(8,128)S(1)} %get-tuple-element.38), channel_id=1, source_target_pairs={{0,1},{1,2},{2,3},{3,0},{4,5},{5,6},{6,7},{7,4},{8,9},{9,10},{10,1... | collective-permute-start | bytes 983048 | tf_op jit(solution)/shard_map/ppermute | solution.py:484
  21.6 0.0 copy-done.2
  21.6 0.0 copy-done.4
  21.6 0.0 copy-done.6
  21.6 0.0 copy-done.9
  21.6 0.0 copy-done.10
  21.7 9.9 %input_gradient.1 = (bf16[256,2560]{1,0:T(8,128)(2,1)}, f32[40,256]{1,0:T(8,128)}, f32[8,256]{1,0:T(8,128)S(1)}) custom-call(s32[1,1]{1,0:T(1,128)S(6)} %copy.13.tile_ref, bf16[256,2560]{1,0:T(8,128)(2,1)S(1)} %bitcast.15, bf16[256,2560]{1,0:T(8,128)(2,1)S(1)} %bitcast.18, f32[40,256]{1,0:T(8,128)S(1)} %get-tuple-element.26.run_ref, ...), custom_call_target="tpu_custom_call" | custom-call | flops 6000000000 | bytes 8000000 | tf_op jit(solution)/shard_map/input_gradient/pallas_call | solution.py:399
  31.6 0.0 collective-permute-done.5
  31.6 0.0 collective-permute-done.4
  31.6 0.4 collective-permute-done.3
  32.0 0.1 add_add_fusion
  32.2 3.1 %collective-permute-start.8 = (f32[80,256]{1,0:T(8,128)S(1)}, f32[80,256]{1,0:T(8,128)S(1)}, u32[]{:S(2)}, u32[]{:S(2)}) collective-permute-start(f32[80,256]{1,0:T(8,128)S(1)} %get-tuple-element.48), channel_id=1, source_target_pairs={{0,12},{1,13},{2,14},{3,15},{4,0},{5,1},{6,2},{7,3},{8,4},{9,5},{1... | collective-permute-start | bytes 245768 | tf_op jit(solution)/shard_map/ppermute | solution.py:484
  35.3 0.0 collective-permute-start.6
  35.3 2.2 %collective-permute-start.7 = (f32[80,256]{1,0:T(8,128)S(1)}, f32[80,256]{1,0:T(8,128)S(1)}, u32[]{:S(2)}, u32[]{:S(2)}) collective-permute-start(f32[80,256]{1,0:T(8,128)S(1)} %get-tuple-element.47), channel_id=1, source_target_pairs={{0,8},{1,9},{2,10},{3,11},{4,12},{5,13},{6,14},{7,15},{8,0},{9,1},... | collective-permute-start | bytes 245768 | tf_op jit(solution)/shard_map/ppermute | solution.py:484
  37.5 0.0 collective-permute-start.9
  37.5 1.2 %collective-permute-done.9 = f32[8,256]{1,0:T(8,128)S(1)} collective-permute-done((f32[8,256]{1,0:T(8,128)S(1)}, f32[8,256]{1,0:T(8,128)S(1)}, u32[]{:S(2)}, u32[]{:S(2)}) %collective-permute-start.9) | collective-permute-done | bytes 8224 | tf_op jit(solution)/shard_map/ppermute | solution.py:492
  38.6 0.0 collective-permute-done.8
  38.7 3.1 %collective-permute-done.6 = f32[80,256]{1,0:T(8,128)S(1)} collective-permute-done((f32[80,256]{1,0:T(8,128)S(1)}, f32[80,256]{1,0:T(8,128)S(1)}, u32[]{:S(2)}, u32[]{:S(2)}) %collective-permute-start.6) | collective-permute-done | bytes 81952 | tf_op jit(solution)/shard_map/ppermute | solution.py:484
  41.8 0.0 collective-permute-done.7
  41.8 0.2 collective-permute-start.10
  42.0 4.4 %collective-permute-done.10 = f32[88,256]{1,0:T(8,128)S(1)} collective-permute-done((f32[88,256]{1,0:T(8,128)S(1)}, f32[88,256]{1,0:T(8,128)S(1)}, u32[]{:S(2)}, u32[]{:S(2)}) %collective-permute-start.10) | collective-permute-done | bytes 90144 | tf_op jit(solution)/shard_map/ppermute | solution.py:488
  46.5 3.4 %collective-permute-start.11 = (f32[88,256]{1,0:T(8,128)S(1)}, f32[88,256]{1,0:T(8,128)S(1)}, u32[]{:S(2)}, u32[]{:S(2)}) collective-permute-start(f32[88,256]{1,0:T(8,128)S(1)} %fusion), channel_id=1, source_target_pairs={{0,32},{1,33},{2,34},{3,35},{4,36},{5,37},{6,38},{7,39},{8,40},{9,... | collective-permute-start | bytes 270344 | tf_op jit(solution)/shard_map/ppermute | solution.py:488
  49.9 3.0 %collective-permute-done.11 = f32[88,256]{1,0:T(8,128)S(1)} collective-permute-done((f32[88,256]{1,0:T(8,128)S(1)}, f32[88,256]{1,0:T(8,128)S(1)}, u32[]{:S(2)}, u32[]{:S(2)}) %collective-permute-start.11) | collective-permute-done | bytes 90144 | tf_op jit(solution)/shard_map/ppermute | solution.py:488
  52.9 6.1 %collective-permute-start.12 = (f32[88,256]{1,0:T(8,128)S(1)}, f32[88,256]{1,0:T(8,128)S(1)}, u32[]{:S(2)}, u32[]{:S(2)}) collective-permute-start(f32[88,256]{1,0:T(8,128)S(1)} %add.92), channel_id=1, source_target_pairs={{0,96},{1,97},{2,98},{3,99},{4,100},{5,101},{6,102},{7,103},{8,104... | collective-permute-start | bytes 270344 | tf_op jit(solution)/shard_map/ppermute | solution.py:488
  59.0 3.1 %collective-permute-done.12 = f32[88,256]{1,0:T(8,128)S(1)} collective-permute-done((f32[88,256]{1,0:T(8,128)S(1)}, f32[88,256]{1,0:T(8,128)S(1)}, u32[]{:S(2)}, u32[]{:S(2)}) %collective-permute-start.12) | collective-permute-done | bytes 90144 | tf_op jit(solution)/shard_map/ppermute | solution.py:488
  62.1 0.1 broadcast_in_dim.19
  62.2 20.6 %all_to_all.5.pieces_ref = f32[16,88,256]{2,1,0:T(8,128)S(1)} all-to-all(f32[16,88,256]{2,1,0:T(8,128)S(1)} %broadcast_in_dim.19), channel_id=1, replica_groups={{0,1,2,3,4,5,6,7,8,9,10,11,12,13,14,15},{16,17,18,19,20,21,22,23,24,25,..., dimensions={0} | all-to-all | bytes 2883584 | tf_op jit(solution)/shard_map/all_to_all | solution.py:518
  82.9 1.6 %weight_rows.1 = (f32[16,80,256]{2,1,0:T(8,128)}, f32[1,20]{1,0:T(1,128)}, f32[1,20]{1,0:T(1,128)}) custom-call(f32[16,88,256]{2,1,0:T(8,128)S(1)} %all_to_all.5.pieces_ref), custom_call_target="tpu_custom_call" | custom-call | flops 10000 | bytes 2600000 | tf_op jit(solution)/shard_map/weight_rows/pallas_call | solution.py:454
  (7 shorter events, 0.1 us)
Async XLA Ops:
  1.3 0.8 copy-start.5
  2.1 0.7 copy-start.7
  2.7 6.0 %copy-start.1 = (bf16[1,256,2560]{2,1,0:T(8,128)(2,1)S(1)}, bf16[1,256,2560]{2,1,0:T(8,128)(2,1)}, u32[]{:S(2)}) copy-start(bf16[1,256,2560]{2,1,0:T(8,128)(2,1)} %param.9) | copy-start | bytes 3932164
  2.7 6.0 %copy-start.3 = (bf16[1,256,2560]{2,1,0:T(8,128)(2,1)S(1)}, bf16[1,256,2560]{2,1,0:T(8,128)(2,1)}, u32[]{:S(2)}) copy-start(bf16[1,256,2560]{2,1,0:T(8,128)(2,1)} %param.10) | copy-start | bytes 3932164
  8.1 3.6 %copy-start.8 = (f32[5,256,8]{2,1,0:T(8,128)}, f32[5,256,8]{2,1,0:T(8,128)S(1)}, u32[]{:S(2)}) copy-start(f32[5,256,8]{2,1,0:T(8,128)S(1)} %get-tuple-element.27.cols_ref) | copy-start | bytes 122884
  8.1 4.0 %collective-permute-start = (f32[128,2560]{1,0:T(8,128)S(1)}, f32[128,2560]{1,0:T(8,128)S(1)}, u32[]{:S(2)}, u32[]{:S(2)}) collective-permute-start(f32[128,2560]{1,0:T(8,128)S(1)} %get-tuple-element.30), channel_id=1, source_target_pairs={{0,128},{128,0},{1,129},{129,1},{2,130},{130,2},{3,131},{131,3},{4... | collective-permute-start | bytes 3932168 | tf_op jit(solution)/shard_map/ppermute | solution.py:492
  8.2 5.2 %collective-permute-start.2 = (f32[256,1280]{1,0:T(8,128)}, f32[256,1280]{1,0:T(8,128)}, u32[]{:S(2)}, u32[]{:S(2)}) collective-permute-start(f32[256,1280]{1,0:T(8,128)} %get-tuple-element.36), channel_id=1, source_target_pairs={{0,128},{128,0},{1,129},{129,1},{2,130},{130,2},{3,131},{131,3},{4... | collective-permute-start | bytes 3932168 | tf_op jit(solution)/shard_map/ppermute | solution.py:492
  12.1 2.7 %copy-start = (bf16[1,256,2560]{2,1,0:T(8,128)(2,1)S(1)}, bf16[1,256,2560]{2,1,0:T(8,128)(2,1)}, u32[]{:S(2)}) copy-start(bf16[1,256,2560]{2,1,0:T(8,128)(2,1)} %param.8) | copy-start | bytes 3932164
  13.2 1.6 %collective-permute-start.1 = (f32[256,256]{1,0:T(8,128)S(1)}, f32[256,256]{1,0:T(8,128)S(1)}, u32[]{:S(2)}, u32[]{:S(2)}) collective-permute-start(f32[256,256]{1,0:T(8,128)S(1)} %proj_gradient.1.grad_ref), channel_id=1, source_target_pairs={{0,128},{128,0},{1,129},{129,1},{2,130},{130,2},{3,131},{131,3},{4... | collective-permute-start | bytes 786440 | tf_op jit(solution)/shard_map/ppermute | solution.py:492
  13.4 8.3 %copy-start.2 = (bf16[1,256,2560]{2,1,0:T(8,128)(2,1)S(1)}, bf16[1,256,2560]{2,1,0:T(8,128)(2,1)}, u32[]{:S(2)}) copy-start(bf16[1,256,2560]{2,1,0:T(8,128)(2,1)} %param.9) | copy-start | bytes 3932164
  13.4 8.3 %copy-start.4 = (bf16[1,256,2560]{2,1,0:T(8,128)(2,1)S(1)}, bf16[1,256,2560]{2,1,0:T(8,128)(2,1)}, u32[]{:S(2)}) copy-start(bf16[1,256,2560]{2,1,0:T(8,128)(2,1)} %param.10) | copy-start | bytes 3932164
  13.4 8.3 %copy-start.6 = (f32[1,40,256]{2,1,0:T(8,128)S(1)}, f32[1,40,256]{2,1,0:T(8,128)}, u32[]{:S(2)}) copy-start(f32[1,40,256]{2,1,0:T(8,128)} %param.11) | copy-start | bytes 122884
  13.4 8.3 %copy-start.9 = (f32[5,256,8]{2,1,0:T(8,128)S(1)}, f32[5,256,8]{2,1,0:T(8,128)}, u32[]{:S(2)}) copy-start(f32[5,256,8]{2,1,0:T(8,128)} %copy-done.8) | copy-start | bytes 122884
  13.4 8.2 %copy-start.10 = (f32[40]{0:T(128)S(1)}, f32[40]{0:T(128)}, u32[]{:S(2)}) copy-start(f32[40]{0:T(128)} %param.14) | copy-start | bytes 484
  17.1 14.5 %collective-permute-start.5 = (f32[320,256]{1,0:T(8,128)S(1)}, f32[320,256]{1,0:T(8,128)S(1)}, u32[]{:S(2)}, u32[]{:S(2)}) collective-permute-start(f32[320,256]{1,0:T(8,128)S(1)} %get-tuple-element.40), channel_id=1, source_target_pairs={{0,3},{1,0},{2,1},{3,2},{4,7},{5,4},{6,5},{7,6},{8,11},{9,8},{10,9... | collective-permute-start | bytes 983048 | tf_op jit(solution)/shard_map/ppermute | solution.py:484
  19.9 11.7 %collective-permute-start.4 = (f32[320,256]{1,0:T(8,128)S(1)}, f32[320,256]{1,0:T(8,128)S(1)}, u32[]{:S(2)}, u32[]{:S(2)}) collective-permute-start(f32[320,256]{1,0:T(8,128)S(1)} %get-tuple-element.39), channel_id=1, source_target_pairs={{0,2},{1,3},{2,0},{3,1},{4,6},{5,7},{6,4},{7,5},{8,10},{9,11},{10,... | collective-permute-start | bytes 983048 | tf_op jit(solution)/shard_map/ppermute | solution.py:484
  20.7 11.3 %collective-permute-start.3 = (f32[320,256]{1,0:T(8,128)S(1)}, f32[320,256]{1,0:T(8,128)S(1)}, u32[]{:S(2)}, u32[]{:S(2)}) collective-permute-start(f32[320,256]{1,0:T(8,128)S(1)} %get-tuple-element.38), channel_id=1, source_target_pairs={{0,1},{1,2},{2,3},{3,0},{4,5},{5,6},{6,7},{7,4},{8,9},{9,10},{10,1... | collective-permute-start | bytes 983048 | tf_op jit(solution)/shard_map/ppermute | solution.py:484
  32.2 6.5 %collective-permute-start.8 = (f32[80,256]{1,0:T(8,128)S(1)}, f32[80,256]{1,0:T(8,128)S(1)}, u32[]{:S(2)}, u32[]{:S(2)}) collective-permute-start(f32[80,256]{1,0:T(8,128)S(1)} %get-tuple-element.48), channel_id=1, source_target_pairs={{0,12},{1,13},{2,14},{3,15},{4,0},{5,1},{6,2},{7,3},{8,4},{9,5},{1... | collective-permute-start | bytes 245768 | tf_op jit(solution)/shard_map/ppermute | solution.py:484
  35.3 6.5 %collective-permute-start.6 = (f32[80,256]{1,0:T(8,128)S(1)}, f32[80,256]{1,0:T(8,128)S(1)}, u32[]{:S(2)}, u32[]{:S(2)}) collective-permute-start(f32[80,256]{1,0:T(8,128)S(1)} %get-tuple-element.49), channel_id=1, source_target_pairs={{0,4},{1,5},{2,6},{3,7},{4,8},{5,9},{6,10},{7,11},{8,12},{9,13},{1... | collective-permute-start | bytes 245768 | tf_op jit(solution)/shard_map/ppermute | solution.py:484
  35.3 6.5 %collective-permute-start.7 = (f32[80,256]{1,0:T(8,128)S(1)}, f32[80,256]{1,0:T(8,128)S(1)}, u32[]{:S(2)}, u32[]{:S(2)}) collective-permute-start(f32[80,256]{1,0:T(8,128)S(1)} %get-tuple-element.47), channel_id=1, source_target_pairs={{0,8},{1,9},{2,10},{3,11},{4,12},{5,13},{6,14},{7,15},{8,0},{9,1},... | collective-permute-start | bytes 245768 | tf_op jit(solution)/shard_map/ppermute | solution.py:484
  37.5 1.2 %collective-permute-start.9 = (f32[8,256]{1,0:T(8,128)S(1)}, f32[8,256]{1,0:T(8,128)S(1)}, u32[]{:S(2)}, u32[]{:S(2)}) collective-permute-start(f32[8,256]{1,0:T(8,128)S(1)} %get-tuple-element.43), channel_id=1, source_target_pairs={{0,128},{128,0},{1,129},{129,1},{2,130},{130,2},{3,131},{131,3},{4... | collective-permute-start | bytes 24584 | tf_op jit(solution)/shard_map/ppermute | solution.py:492
  41.8 4.6 %collective-permute-start.10 = (f32[88,256]{1,0:T(8,128)S(1)}, f32[88,256]{1,0:T(8,128)S(1)}, u32[]{:S(2)}, u32[]{:S(2)}) collective-permute-start(f32[88,256]{1,0:T(8,128)S(1)} %pad_maximum_fusion), channel_id=1, source_target_pairs={{0,16},{1,17},{2,18},{3,19},{4,20},{5,21},{6,22},{7,23},{8,24},{9,... | collective-permute-start | bytes 270344 | tf_op jit(solution)/shard_map/ppermute | solution.py:488
  46.5 6.4 %collective-permute-start.11 = (f32[88,256]{1,0:T(8,128)S(1)}, f32[88,256]{1,0:T(8,128)S(1)}, u32[]{:S(2)}, u32[]{:S(2)}) collective-permute-start(f32[88,256]{1,0:T(8,128)S(1)} %fusion), channel_id=1, source_target_pairs={{0,32},{1,33},{2,34},{3,35},{4,36},{5,37},{6,38},{7,39},{8,40},{9,... | collective-permute-start | bytes 270344 | tf_op jit(solution)/shard_map/ppermute | solution.py:488
  52.9 9.2 %collective-permute-start.12 = (f32[88,256]{1,0:T(8,128)S(1)}, f32[88,256]{1,0:T(8,128)S(1)}, u32[]{:S(2)}, u32[]{:S(2)}) collective-permute-start(f32[88,256]{1,0:T(8,128)S(1)} %add.92), channel_id=1, source_target_pairs={{0,96},{1,97},{2,98},{3,99},{4,100},{5,101},{6,102},{7,103},{8,104... | collective-permute-start | bytes 270344 | tf_op jit(solution)/shard_map/ppermute | solution.py:488
